TPU v7x, 32 devices: a whole 2x2x4 slice. The times are simulated.
32 devices in a mesh: dp: 8 (over z, x), tensor: 4 (over y, core).
Axes of the slice: x: 2, y: 2, z: 4, core: 2. Of those that a mesh axis runs over, the one named last changes fastest.
Arguments:
- tokens: bfloat16 [16, 4, 128, 1024], P(None, 'tensor', 'dp'), may hold values from -6 to 6
- grad_output: bfloat16 [16, 4, 128, 1024], P(None, 'tensor', 'dp'), may hold values from -6 to 6
- query_weight: bfloat16 [1024, 1024], P('dp', 'tensor'), may hold values from -0.1875 to 0.1875
- key_weight: bfloat16 [1024, 1024], P('dp', 'tensor'), may hold values from -0.1875 to 0.1875
- value_weight: bfloat16 [1024, 1024], P('dp', 'tensor'), may hold values from -0.1875 to 0.1875
- rates_weight: bfloat16 [1024, 24], P('dp', 'tensor'), may hold values from -0.1875 to 0.1875
- out_weight: bfloat16 [1024, 1024], P('dp', 'tensor'), may hold values from -0.75 to 0.75
- gate_weight: bfloat16 [1024, 2816], P('dp', 'tensor'), may hold values from -0.1875 to 0.1875
- up_weight: bfloat16 [1024, 2816], P('dp', 'tensor'), may hold values from -0.1875 to 0.1875
- down_weight: bfloat16 [1024, 2816], P('dp', 'tensor'), may hold values from -0.109375 to 0.109375
- norm1_gain: bfloat16 [1024], P('dp'), may hold values from 0.5 to 1.5
- norm2_gain: bfloat16 [1024], P('dp'), may hold values from 0.5 to 1.5
- persist_key: bfloat16 [8, 16, 128], P('tensor'), may hold values from -5 to 5
- persist_value: bfloat16 [8, 16, 128], P('tensor'), may hold values from -5 to 5
- memory_first: float32 [8, 128, 128], P('tensor'), may hold values from -0.5 to 0.5
- memory_second: float32 [8, 128, 128], P('tensor'), may hold values from -0.5 to 0.5
- seq_lengths: int32 [16], replicated, may hold values from 256 to 512, as said below
- deal: int32 [16], replicated, may hold values from 0 to 15, each once
Outputs:
- layer_out: bfloat16 [16, 4, 128, 1024], P(None, 'tensor', 'dp')
- grad_tokens: bfloat16 [16, 4, 128, 1024], P(None, 'tensor', 'dp')
- grad_query: float32 [1024, 1024], P('dp', 'tensor')
- grad_key: float32 [1024, 1024], P('dp', 'tensor')
- grad_value: float32 [1024, 1024], P('dp', 'tensor')
- grad_rates: float32 [1024, 24], P('dp', 'tensor')
- grad_out: float32 [1024, 1024], P('dp', 'tensor')
- grad_gate: float32 [1024, 2816], P('dp', 'tensor')
- grad_up: float32 [1024, 2816], P('dp', 'tensor')
- grad_down: float32 [1024, 2816], P('dp', 'tensor')
- grad_norm1: float32 [1024], replicated
- grad_norm2: float32 [1024], replicated
- grad_persist_key: float32 [8, 16, 128], P('tensor')
- grad_persist_value: float32 [8, 16, 128], P('tensor')
- grad_memory_first: float32 [8, 128, 128], P('tensor')
- grad_memory_second: float32 [8, 128, 128], P('tensor')
Inputs may be any that keep to these rules, and one draw needn't show every extreme that they name: `seq_lengths`: at least one sequence has 512 tokens; slots at and past a sequence's length are padding. A permutation; sequence s is in micro-batch deal[s] // 8 and is handled by dp device deal[s] % 8.
All inputs are finite; a program needn't handle non-finite values.
Results may differ from a plain program's by a relative error of at most 0.017.
Values may be sent and summed in bfloat16 or wider, within the bound.
No kernel may reach another device: no remote copies, remote signals or barrier semaphores. Data moves between devices by JAX's collectives and lax.ppermute only.
A program may use at most 192 MiB of HBM per device.

v0:
```python
from functools import partial

import jax
import jax.numpy as jnp
from jax import lax
from jax.sharding import PartitionSpec as P

CH = 64
WINDOW = 256
QB = 512


def highest(left, right):
    return jnp.dot(left, right, precision=lax.Precision.HIGHEST, preferred_element_type=jnp.float32)


def row_norm(values_in):
    return values_in * lax.rsqrt(jnp.mean(values_in * values_in, axis=-1, keepdims=True) + 1e-06)


def memory_span(carry_in, pieces):
    first_layer, second_layer, moment_first, moment_second = carry_in
    span_keys, span_values, span_queries, span_rates, span_live = pieces
    recalled = highest(jax.nn.silu(highest(span_queries, first_layer)), second_layer)
    pre_act = highest(span_keys, first_layer)
    sigmoid_pre = jax.nn.sigmoid(pre_act)
    activated = pre_act * sigmoid_pre
    mismatch = highest(activated, second_layer) - span_values
    weighting = 2.0 * span_rates[:, 0] * span_live / (span_live.shape[0] * span_keys.shape[1])
    mismatch_grad = mismatch * weighting[:, None]
    grad_second = highest(activated.T, mismatch_grad)
    grad_pre = (
        highest(mismatch_grad, second_layer.T) * sigmoid_pre * (1.0 + pre_act * (1.0 - sigmoid_pre))
    )
    grad_first = highest(span_keys.T, grad_pre)
    momentum = jnp.mean(span_rates[:, 1])
    forget = 0.5 * jnp.mean(span_rates[:, 2])
    moment_first = momentum * moment_first - grad_first
    moment_second = momentum * moment_second - grad_second
    first_layer = (1.0 - forget) * first_layer + moment_first
    second_layer = (1.0 - forget) * second_layer + moment_second
    return ((first_layer, second_layer, moment_first, moment_second), recalled)


def head_mix(
    queries,
    keys,
    values,
    rates,
    persist_keys,
    persist_values,
    first_layer,
    second_layer,
    length,
    span_len,
    window,
    block_rows,
):
    row_total = queries.shape[0]
    spans = row_total // span_len
    live_rows = (jnp.arange(row_total, dtype=jnp.int32) < length).astype(jnp.float32)

    def grouped(tensor_in):
        return tensor_in.reshape((spans, span_len) + tensor_in.shape[1:])

    blank_first = jnp.zeros_like(first_layer)
    blank_second = jnp.zeros_like(second_layer)
    carried, recalled = lax.scan(
        jax.checkpoint(memory_span),
        (first_layer, second_layer, blank_first, blank_second),
        (
            grouped(row_norm(keys)),
            grouped(values),
            grouped(row_norm(queries)),
            grouped(rates),
            grouped(live_rows),
        ),
    )
    recalled = recalled.reshape(row_total, -1)
    padded_keys = jnp.pad(keys, ((window, 0), (0, 0)))
    padded_values = jnp.pad(values, ((window, 0), (0, 0)))
    starts = jnp.arange(row_total // block_rows) * block_rows
    groups = block_rows // span_len

    def attend(block_start):
        scaled = queries * queries.shape[1] ** (-0.5)
        near_recalled = recalled.reshape(groups, span_len, -1)
        positions = block_start + jnp.arange(block_rows, dtype=jnp.int32)
        key_positions = block_start - window + jnp.arange(block_rows + window, dtype=jnp.int32)
        near_ok = (
            (key_positions[None, :] <= positions[:, None])
            & (key_positions[None, :] > positions[:, None] - window)
            & (key_positions[None, :] >= 0)
        )
        recall_ok = (positions < length).reshape(groups, 1, span_len)
        persist_scores = highest(scaled, persist_keys.T)
        near_scores = jnp.where(near_ok, highest(scaled, padded_keys.T), -1e30)
        recall_scores = jnp.where(
            recall_ok,
            jnp.einsum(
                "gqd,gkd->gqk",
                scaled.reshape(groups, span_len, -1),
                near_recalled,
                precision=lax.Precision.HIGHEST,
            ),
            -1e30,
        )
        top_rows = jnp.maximum(
            jnp.maximum(jnp.max(persist_scores, axis=1), jnp.max(near_scores, axis=1)),
            jnp.max(recall_scores, axis=2).reshape(block_rows),
        )
        persist_exp = jnp.exp(persist_scores - top_rows[:, None])
        near_exp = jnp.exp(near_scores - top_rows[:, None])
        recall_exp = jnp.exp(recall_scores - top_rows.reshape(groups, span_len, 1))
        denominator = (
            jnp.sum(persist_exp, axis=1)
            + jnp.sum(near_exp, axis=1)
            + jnp.sum(recall_exp, axis=2).reshape(block_rows)
        )
        weighted = highest(persist_exp, persist_values) + highest(near_exp, padded_values)
        weighted = weighted + jnp.einsum(
            "gqk,gkd->gqd", recall_exp, near_recalled, precision=lax.Precision.HIGHEST
        ).reshape(block_rows, -1)
        return weighted / denominator[:, None]

    return lax.map(jax.checkpoint(attend), starts).reshape(row_total, -1)


def mix_heads(
    queries,
    keys,
    values,
    logits,
    persist_keys,
    persist_values,
    first_layer,
    second_layer,
    length,
    span_len,
    window,
    block_rows,
):
    row_total = queries.shape[0]
    head_count = persist_keys.shape[0]

    def by_head(tensor_in):
        return tensor_in.reshape(row_total, head_count, -1).transpose(1, 0, 2)

    per_head = partial(
        head_mix, length=length, span_len=span_len, window=window, block_rows=block_rows
    )
    outputs = jax.vmap(per_head)(
        by_head(queries),
        by_head(keys),
        by_head(values),
        by_head(jax.nn.sigmoid(logits)),
        persist_keys,
        persist_values,
        first_layer,
        second_layer,
    )
    return outputs.transpose(1, 0, 2).reshape(row_total, -1)


def against(left, right):
    return lax.dot_general(
        left, right, (((1,), (1,)), ((), ())), preferred_element_type=jnp.float32
    )


def inner_rows(left, right):
    return lax.dot_general(
        left, right, (((0,), (0,)), ((), ())), preferred_element_type=jnp.float32
    )


def per_device(
    tokens,
    grad_output,
    query_weight,
    key_weight,
    value_weight,
    rates_weight,
    out_weight,
    gate_weight,
    up_weight,
    down_weight,
    norm1_gain,
    norm2_gain,
    persist_key,
    persist_value,
    memory_first,
    memory_second,
    seq_lengths,
    deal,
):
    devices = lax.axis_size("dp")
    dp_index = lax.axis_index("dp")
    tensor_index = lax.axis_index("tensor")
    seq_count = seq_lengths.shape[0]
    batches = seq_count // devices
    local_rows = tokens.shape[2]
    model_width = tokens.shape[3]
    quarter = local_rows * devices
    slot_ids = jnp.arange(seq_count, dtype=jnp.int32)
    slot_seq = jnp.sum(jnp.where(deal[None, :] == slot_ids[:, None], slot_ids[None, :], 0), axis=1)
    batch_of = deal // devices
    batch_ids = jnp.arange(batches, dtype=jnp.int32)
    batch_tokens = jnp.sum(
        jnp.where(batch_of[None, :] == batch_ids[:, None], seq_lengths[None, :], 0), axis=1
    ).astype(jnp.float32)
    batch_scale = jnp.sum(seq_lengths).astype(jnp.float32) / (batches * batch_tokens)
    (
        query_full,
        key_full,
        value_full,
        rates_full,
        out_full,
        gate_full,
        up_full,
        down_full,
        gain_first,
        gain_second,
    ) = (
        lax.all_gather(query_weight, "dp", axis=0, tiled=True),
        lax.all_gather(key_weight, "dp", axis=0, tiled=True),
        lax.all_gather(value_weight, "dp", axis=0, tiled=True),
        lax.all_gather(rates_weight, "dp", axis=0, tiled=True),
        lax.all_gather(out_weight, "dp", axis=0, tiled=True),
        lax.all_gather(gate_weight, "dp", axis=0, tiled=True),
        lax.all_gather(up_weight, "dp", axis=0, tiled=True),
        lax.all_gather(down_weight, "dp", axis=0, tiled=True),
        lax.all_gather(norm1_gain, "dp", axis=0, tiled=True),
        lax.all_gather(norm2_gain, "dp", axis=0, tiled=True),
    )
    project_weight = jnp.concatenate([query_full, key_full, value_full], axis=1)
    head_width = query_full.shape[1]
    gain_one = gain_first.astype(jnp.float32)
    gain_two = gain_second.astype(jnp.float32)
    persist_keys = persist_key.astype(jnp.float32)
    persist_values = persist_value.astype(jnp.float32)
    layer_out = jnp.zeros(tokens.shape, jnp.bfloat16)
    grad_tokens = jnp.zeros(tokens.shape, jnp.bfloat16)
    weight_totals = None
    memory_totals = None
    gain1_total = jnp.zeros((model_width,), jnp.float32)
    gain2_total = jnp.zeros((model_width,), jnp.float32)
    for batch_index in range(batches):
        seq_pick = slot_seq[batch_index * devices : (batch_index + 1) * devices]
        got_tokens, got_cots = (
            lax.all_to_all(tokens[seq_pick, 0], "dp", split_axis=0, concat_axis=0, tiled=True),
            lax.all_to_all(grad_output[seq_pick, 0], "dp", split_axis=0, concat_axis=0, tiled=True),
        )
        token_rows = got_tokens.reshape(quarter, model_width).astype(jnp.float32)
        my_seq = slot_seq[batch_index * devices + dp_index]
        length = seq_lengths[my_seq]
        positions = tensor_index * quarter + jnp.arange(quarter, dtype=jnp.int32)
        live_mask = (positions < length).astype(jnp.float32)[:, None]
        inverse_first = lax.rsqrt(jnp.mean(token_rows * token_rows, axis=-1, keepdims=True) + 1e-06)
        normed_first = token_rows * inverse_first
        full_first = lax.all_gather(
            (normed_first * gain_one).astype(jnp.bfloat16), "tensor", axis=0, tiled=True
        )
        projected = jnp.dot(full_first, project_weight, preferred_element_type=jnp.float32)
        rate_logits = jnp.dot(full_first, rates_full, preferred_element_type=jnp.float32)

        def local_mix(
            query_part,
            key_part,
            value_part,
            logit_part,
            pkey_part,
            pvalue_part,
            first_part,
            second_part,
        ):
            return mix_heads(
                query_part,
                key_part,
                value_part,
                logit_part,
                pkey_part,
                pvalue_part,
                first_part,
                second_part,
                length,
                CH,
                WINDOW,
                QB,
            )

        mixed, mix_pullback = jax.vjp(
            local_mix,
            projected[:, :head_width],
            projected[:, head_width : 2 * head_width],
            projected[:, 2 * head_width :],
            rate_logits,
            persist_keys,
            persist_values,
            memory_first,
            memory_second,
        )
        mixed_low = mixed.astype(jnp.bfloat16)
        attended = lax.psum_scatter(
            against(mixed_low, out_full).astype(jnp.bfloat16),
            "tensor",
            scatter_dimension=0,
            tiled=True,
        ).astype(jnp.float32)
        residual = token_rows + attended
        inverse_second = lax.rsqrt(jnp.mean(residual * residual, axis=-1, keepdims=True) + 1e-06)
        normed_second = residual * inverse_second
        full_second = lax.all_gather(
            (normed_second * gain_two).astype(jnp.bfloat16), "tensor", axis=0, tiled=True
        )
        gate_pre = jnp.dot(full_second, gate_full, preferred_element_type=jnp.float32)
        up_pre = jnp.dot(full_second, up_full, preferred_element_type=jnp.float32)
        gate_sig = jax.nn.sigmoid(gate_pre)
        hidden = (gate_pre * gate_sig * up_pre).astype(jnp.bfloat16)
        feed_rows = lax.psum_scatter(
            against(hidden, down_full).astype(jnp.bfloat16),
            "tensor",
            scatter_dimension=0,
            tiled=True,
        ).astype(jnp.float32)
        out_rows = live_mask * (residual + feed_rows)
        cot_rows = (
            got_cots.reshape(quarter, model_width).astype(jnp.float32)
            * batch_scale[batch_index]
            * live_mask
        )
        cot_full = lax.all_gather(cot_rows.astype(jnp.bfloat16), "tensor", axis=0, tiled=True)
        hidden_grad = jnp.dot(cot_full, down_full, preferred_element_type=jnp.float32)
        down_step = inner_rows(cot_full, hidden)
        gate_grad = (hidden_grad * up_pre * gate_sig * (1.0 + gate_pre * (1.0 - gate_sig))).astype(
            jnp.bfloat16
        )
        up_grad = (hidden_grad * gate_pre * gate_sig).astype(jnp.bfloat16)
        gate_step = inner_rows(full_second, gate_grad)
        up_step = inner_rows(full_second, up_grad)
        normed_two_grad = lax.psum_scatter(
            (against(gate_grad, gate_full) + against(up_grad, up_full)).astype(jnp.bfloat16),
            "tensor",
            scatter_dimension=0,
            tiled=True,
        ).astype(jnp.float32)
        gain2_total = gain2_total + jnp.sum(normed_two_grad * normed_second, axis=0)
        scaled_two = normed_two_grad * gain_two
        residual_grad = cot_rows + inverse_second * (
            scaled_two
            - normed_second * jnp.mean(scaled_two * normed_second, axis=-1, keepdims=True)
        )
        mixer_cot = lax.all_gather(residual_grad.astype(jnp.bfloat16), "tensor", axis=0, tiled=True)
        mixed_grad = jnp.dot(mixer_cot, out_full, preferred_element_type=jnp.float32)
        out_step = inner_rows(mixer_cot, mixed_low)
        (
            query_grad,
            key_grad,
            value_grad,
            logit_grad,
            pkey_grad,
            pvalue_grad,
            first_grad,
            second_grad,
        ) = mix_pullback(mixed_grad)
        project_grad = jnp.concatenate([query_grad, key_grad, value_grad], axis=1).astype(
            jnp.bfloat16
        )
        logit_low = logit_grad.astype(jnp.bfloat16)
        project_step = inner_rows(full_first, project_grad)
        rates_step = inner_rows(full_first, logit_low)
        normed_one_grad = lax.psum_scatter(
            (against(project_grad, project_weight) + against(logit_low, rates_full)).astype(
                jnp.bfloat16
            ),
            "tensor",
            scatter_dimension=0,
            tiled=True,
        ).astype(jnp.float32)
        gain1_total = gain1_total + jnp.sum(normed_one_grad * normed_first, axis=0)
        scaled_one = normed_one_grad * gain_one
        token_grad = residual_grad + inverse_first * (
            scaled_one - normed_first * jnp.mean(scaled_one * normed_first, axis=-1, keepdims=True)
        )
        back_out, back_grad = (
            lax.all_to_all(
                out_rows.astype(jnp.bfloat16).reshape(devices, local_rows, model_width),
                "dp",
                split_axis=0,
                concat_axis=0,
                tiled=True,
            ),
            lax.all_to_all(
                token_grad.astype(jnp.bfloat16).reshape(devices, local_rows, model_width),
                "dp",
                split_axis=0,
                concat_axis=0,
                tiled=True,
            ),
        )
        layer_out = layer_out.at[seq_pick, 0].set(back_out)
        grad_tokens = grad_tokens.at[seq_pick, 0].set(back_grad)
        batch_steps = (
            project_step[:, :head_width],
            project_step[:, head_width : 2 * head_width],
            project_step[:, 2 * head_width :],
            rates_step,
            out_step,
            gate_step,
            up_step,
            down_step,
        )
        weight_totals = (
            batch_steps
            if weight_totals is None
            else jax.tree.map(jnp.add, weight_totals, batch_steps)
        )
        memory_steps = (pkey_grad, pvalue_grad, first_grad, second_grad)
        memory_totals = (
            memory_steps
            if memory_totals is None
            else jax.tree.map(jnp.add, memory_totals, memory_steps)
        )
    weight_totals = (
        lax.psum_scatter(weight_totals[0], "dp", scatter_dimension=0, tiled=True),
        lax.psum_scatter(weight_totals[1], "dp", scatter_dimension=0, tiled=True),
        lax.psum_scatter(weight_totals[2], "dp", scatter_dimension=0, tiled=True),
        lax.psum_scatter(weight_totals[3], "dp", scatter_dimension=0, tiled=True),
        lax.psum_scatter(weight_totals[4], "dp", scatter_dimension=0, tiled=True),
        lax.psum_scatter(weight_totals[5], "dp", scatter_dimension=0, tiled=True),
        lax.psum_scatter(weight_totals[6], "dp", scatter_dimension=0, tiled=True),
        lax.psum_scatter(weight_totals[7], "dp", scatter_dimension=0, tiled=True),
    )
    memory_summed = lax.psum(
        (memory_totals[0], memory_totals[1], memory_totals[2], memory_totals[3]), "dp"
    )
    gain_summed = lax.psum((gain1_total, gain2_total), ("dp", "tensor"))
    return (
        layer_out,
        grad_tokens,
        weight_totals[0],
        weight_totals[1],
        weight_totals[2],
        weight_totals[3],
        weight_totals[4],
        weight_totals[5],
        weight_totals[6],
        weight_totals[7],
        gain_summed[0],
        gain_summed[1],
        memory_summed[0],
        memory_summed[1],
        memory_summed[2],
        memory_summed[3],
    )


def solution(mesh):
    return jax.shard_map(
        per_device,
        mesh=mesh,
        in_specs=(
            P(None, "tensor", "dp", None),
            P(None, "tensor", "dp", None),
            P("dp", "tensor"),
            P("dp", "tensor"),
            P("dp", "tensor"),
            P("dp", "tensor"),
            P("dp", "tensor"),
            P("dp", "tensor"),
            P("dp", "tensor"),
            P("dp", "tensor"),
            P("dp"),
            P("dp"),
            P("tensor", None, None),
            P("tensor", None, None),
            P("tensor", None, None),
            P("tensor", None, None),
            P(),
            P(),
        ),
        out_specs=(
            P(None, "tensor", "dp", None),
            P(None, "tensor", "dp", None),
            P("dp", "tensor"),
            P("dp", "tensor"),
            P("dp", "tensor"),
            P("dp", "tensor"),
            P("dp", "tensor"),
            P("dp", "tensor"),
            P("dp", "tensor"),
            P("dp", "tensor"),
            P(),
            P(),
            P("tensor", None, None),
            P("tensor", None, None),
            P("tensor", None, None),
            P("tensor", None, None),
        ),
        check_vma=False,
    )
```

profile of v0, /device:TPU:0, one launch (start us, length us, event | category | flops | bytes accessed | tf_op | source)
XLA Modules:
  0.0 1870.3 jit_solution(6306745230003976577)
XLA Ops:
  32.5 20.8 %all-gather = bf16[8,1,128]{2,1,0:T(2,128)(2,1)S(1)} all-gather(bf16[1,1,128]{2,1,0:T(2,128)(2,1)S(1)} %bitcast.964), channel_id=1, replica_groups=mesh['dp'=8,'tensor'=4] {'dp'}, dimensions={0}, use_global_device_ids=true | all-gather | bytes 2304 | tf_op jit(solution)/shard_map/all_gather | solution.py:233
  63.7 31.5 %all_gather.56 = bf16[1024,256]{1,0:T(8,128)(2,1)S(1)} all-gather(bf16[128,256]{1,0:T(8,128)(2,1)S(1)} %copy-done.140), channel_id=1, replica_groups=mesh['dp'=8,'tensor'=4] {'dp'}, dimensions={0}, use_global_device_ids=true | all-gather | bytes 589824 | tf_op jit(solution)/shard_map/all_gather | solution.py:225
  95.3 31.4 %all_gather.57 = bf16[1024,256]{1,0:T(8,128)(2,1)S(1)} all-gather(bf16[128,256]{1,0:T(8,128)(2,1)S(1)} %copy-done.141), channel_id=1, replica_groups=mesh['dp'=8,'tensor'=4] {'dp'}, dimensions={0}, use_global_device_ids=true | all-gather | bytes 589824 | tf_op jit(solution)/shard_map/all_gather | solution.py:226
  129.3 26.0 %all_gather.59 = bf16[1024,6]{0,1:T(8,128)(2,1)S(1)} all-gather(bf16[128,6]{0,1:T(8,128)(2,1)S(1)} %copy-done.205), channel_id=1, replica_groups=mesh['dp'=8,'tensor'=4] {'dp'}, dimensions={0}, use_global_device_ids=true | all-gather | bytes 13824 | tf_op jit(solution)/shard_map/all_gather | solution.py:228
  155.3 31.2 %all_gather.58 = bf16[1024,256]{1,0:T(8,128)(2,1)S(1)} all-gather(bf16[128,256]{1,0:T(8,128)(2,1)S(1)} %copy-done.142), channel_id=1, replica_groups=mesh['dp'=8,'tensor'=4] {'dp'}, dimensions={0}, use_global_device_ids=true | all-gather | bytes 589824 | tf_op jit(solution)/shard_map/all_gather | solution.py:227
  187.5 33.2 %all_gather.60 = bf16[1024,256]{1,0:T(8,128)(2,1)} all-gather(bf16[128,256]{1,0:T(8,128)(2,1)S(1)} %copy-done.143), channel_id=1, replica_groups=mesh['dp'=8,'tensor'=4] {'dp'}, dimensions={0}, use_global_device_ids=true | all-gather | bytes 589824 | tf_op jit(solution)/shard_map/all_gather | solution.py:229
  258.0 83.7 %while.145 = (s32[]{:T(128)}, f32[2,128,128]{2,1,0:T(8,128)S(1)}, f32[2,128,128]{2,1,0:T(8,128)S(1)}, f32[2,128,128]{2,1,0:T(8,128)S(1)}, f32[2,128,128]{2,1,0:T...) while((s32[]{:T(128)}, f32[2,128,128]{2,1,0:T(8,128)S(1)}, ...), condition=%wide.region_26.27_spmd.clone, body=%wide.region_23.26_spmd.clone.sunk | while | flops 176915008 | bytes 3941881 | solution.py:68
  368.5 69.5 %while.144 = (s32[]{:T(128)}, f32[2,128,128]{2,1,0:T(8,128)S(1)}, f32[2,128,128]{2,1,0:T(8,128)S(1)}, f32[2,128,128]{2,1,0:T(8,128)S(1)}, f32[2,128,128]{2,1,0:T...) while((s32[]{:T(128)}, f32[2,128,128]{2,1,0:T(8,128)S(1)}, ...), condition=%wide.region_9.10_spmd.clone, body=%wide.region_6.9_spmd.clone.sunk | while | flops 176915008 | bytes 3941377 | solution.py:68
  527.6 40.7 %all-gather.20.cloned.1.call-done = bf16[1024,704]{0,1:T(8,128)(2,1)} async-done(((bf16[128,704]{0,1:T(8,128)(2,1)}), bf16[1024,704]{0,1:T(8,128)(2,1)}) %all-gather.20.cloned.1.call-update) | async-done | bytes 1441808 | tf_op jit(solution)/shard_map/all_gather | solution.py:231
  585.3 45.2 %all-gather.22.cloned.1.call-done = bf16[1024,704]{0,1:T(8,128)(2,1)} async-done(((bf16[128,704]{0,1:T(8,128)(2,1)}), bf16[1024,704]{0,1:T(8,128)(2,1)}) %all-gather.22.cloned.1.call-update) | async-done | bytes 1441808 | tf_op jit(solution)/shard_map/all_gather | solution.py:232
  640.6 22.0 %reduce-scatter.29.cloned.1.call-done = bf16[128,1024]{1,0:T(8,128)(2,1)} async-done(((bf16[512,1024]{1,0:T(8,128)(2,1)}), bf16[128,1024]{1,0:T(8,128)(2,1)}) %reduce-scatter.29.cloned.1.call-update) | async-done | bytes 262160 | tf_op jit(solution)/shard_map/reduce_scatter | solution.py:341
  739.5 157.3 %while.147 = (s32[]{:T(128)}, f32[2,128,128]{2,1,0:T(8,128)S(1)}, f32[2,128,128]{2,1,0:T(8,128)}, f32[2,128,128]{2,1,0:T(8,128)}, f32[2,128,128]{2,1,0:T(8,128)}...) while((s32[]{:T(128)}, f32[2,128,128]{2,1,0:T(8,128)S(1)}, ...), condition=%wide.region_89.90_spmd.clone, body=%wide.region_81.89_spmd.clone.sunk | while | flops 455378432 | bytes 10772712 | solution.py:68
  950.5 25.4 %reduce-scatter.23.cloned.1.call-done = bf16[128,1024]{1,0:T(8,128)(2,1)} async-done(((bf16[512,1024]{1,0:T(8,128)(2,1)}), bf16[128,1024]{1,0:T(8,128)(2,1)}) %reduce-scatter.23.cloned.1.call-update) | async-done | bytes 262160 | tf_op jit(solution)/shard_map/reduce_scatter | solution.py:320
  975.9 27.4 %reduce-scatter.25.cloned.1.call-done = bf16[128,1024]{1,0:T(8,128)(2,1)} async-done(((bf16[512,1024]{1,0:T(8,128)(2,1)}), bf16[128,1024]{1,0:T(8,128)(2,1)}) %reduce-scatter.25.cloned.1.call-update) | async-done | bytes 262160 | tf_op jit(solution)/shard_map/reduce_scatter | solution.py:341
  1076.1 154.1 %while.146 = (s32[]{:T(128)}, f32[2,128,128]{2,1,0:T(8,128)}, f32[2,128,128]{2,1,0:T(8,128)}, f32[2,128,128]{2,1,0:T(8,128)}, f32[2,128,128]{2,1,0:T(8,128)}, /*...) while((s32[]{:T(128)}, f32[2,128,128]{2,1,0:T(8,128)}, ...), condition=%wide.region_60.61_spmd.clone, body=%wide.region_52.60_spmd.clone.sunk | while | flops 455378432 | bytes 10765488 | solution.py:68
  1345.8 38.1 %all-reduce.13 = (f32[2,16,128]{2,1,0:T(8,128)}, f32[2,16,128]{2,1,0:T(8,128)}) all-reduce(f32[2,16,128]{2,1,0:T(8,128)S(1)} %convolution_add_fusion.36, f32[2,16,128]{2,1,0:T(8,128)S(1)} %convolution_add_fusion.35), channel_id=1, replica_groups=mesh['dp'=8,'tensor'=4] {'dp'}, use_global_device_ids=true, to_apply=%region_109.110 | all-reduce | flops 8192 | bytes 65536 | tf_op jit(solution)/shard_map/psum | solution.py:434
  1384.0 37.8 %all-reduce.12 = (f32[1024]{0:T(1024)}, f32[1024]{0:T(1024)}) all-reduce(f32[1024]{0:T(1024)S(1)} %add.774, f32[1024]{0:T(1024)S(1)} %add.775), channel_id=1, replica_groups=mesh['dp'=8,'tensor'=4] {'dp','tensor'}, use_global_device_ids=true, to_apply=%region_105.106 | all-reduce | flops 2048 | bytes 16384 | tf_op jit(solution)/shard_map/psum | solution.py:437
  1425.9 16.6 reduce-scatter.47.cloned.1.call-done
  1442.5 75.5 %reduce-scatter.45.cloned.1.call-done = f32[128,704]{0,1:T(8,128)} async-done(((f32[1024,704]{0,1:T(8,128)}), f32[128,704]{0,1:T(8,128)}) %reduce-scatter.45.cloned.1.call-update) | async-done | bytes 360464 | tf_op jit(solution)/shard_map/reduce_scatter | solution.py:431
  1518.0 75.4 %reduce-scatter.43.cloned.1.call-done = f32[128,704]{0,1:T(8,128)} async-done(((f32[1024,704]{0,1:T(8,128)}), f32[128,704]{0,1:T(8,128)}) %reduce-scatter.43.cloned.1.call-update) | async-done | bytes 360464 | tf_op jit(solution)/shard_map/reduce_scatter | solution.py:430
  1593.4 66.5 %reduce-scatter.41.cloned.1.call-done = f32[128,256]{1,0:T(8,128)} async-done(((f32[1024,256]{1,0:T(8,128)}), f32[128,256]{1,0:T(8,128)}) %reduce-scatter.41.cloned.1.call-update) | async-done | bytes 131088 | tf_op jit(solution)/shard_map/reduce_scatter | solution.py:429
  1659.9 66.6 %reduce-scatter.33.cloned.1.call-done = f32[128,256]{1,0:T(8,128)} async-done(((f32[1024,256]{1,0:T(8,128)}), f32[128,256]{1,0:T(8,128)}) %reduce-scatter.33.cloned.1.call-update) | async-done | bytes 131088 | tf_op jit(solution)/shard_map/reduce_scatter | solution.py:425
  1726.5 66.2 %reduce-scatter.35.cloned.1.call-done = f32[128,256]{1,0:T(8,128)} async-done(((f32[1024,256]{1,0:T(8,128)}), f32[128,256]{1,0:T(8,128)}) %reduce-scatter.35.cloned.1.call-update) | async-done | bytes 131088 | tf_op jit(solution)/shard_map/reduce_scatter | solution.py:426
  1792.6 66.9 %reduce-scatter.37.cloned.1.call-done = f32[128,256]{1,0:T(8,128)} async-done(((f32[1024,256]{1,0:T(8,128)}), f32[128,256]{1,0:T(8,128)}) %reduce-scatter.37.cloned.1.call-update) | async-done | bytes 131088 | tf_op jit(solution)/shard_map/reduce_scatter | solution.py:427
  (1738 shorter events, 996.9 us)
Async XLA Ops:
  32.5 189.4 %all-gather.14.cloned.1.call-start = ((), (), s32[]{:S(2)}) async-start(), calls=%async_computation.24 | async-start | bytes 1310720 | tf_op jit(solution)/shard_map/all_gather | solution.py:261
  54.8 172.4 %all-gather.24.cloned.1.call-start = ((), (), s32[]{:S(2)}) async-start(), calls=%async_computation.31 | async-start | bytes 1310720 | tf_op jit(solution)/shard_map/all_gather | solution.py:261
  128.0 352.2 %reduce-scatter.21.cloned.1.call-start = ((), (), s32[]{:S(2)}) async-start(), calls=%async_computation.32 | async-start | bytes 1310720 | tf_op jit(solution)/shard_map/reduce_scatter | solution.py:304
  483.2 85.1 %all-gather.20.cloned.1.call-start = ((), (), s32[]{:S(2)}) async-start(), calls=%async_computation.28 | async-start | bytes 1622016 | tf_op jit(solution)/shard_map/all_gather | solution.py:231
  491.6 93.6 %all-gather.32.cloned.1.call-start = ((), (), s32[]{:S(2)}) async-start(), calls=%async_computation.39 | async-start | bytes 1310720 | tf_op jit(solution)/shard_map/all_gather | solution.py:332
  507.6 122.9 %all-gather.22.cloned.1.call-start = ((), (), s32[]{:S(2)}) async-start(), calls=%async_computation.29 | async-start | bytes 1622016 | tf_op jit(solution)/shard_map/all_gather | solution.py:232
  508.3 131.2 %reduce-scatter.17.cloned.1.call-start = ((), (), s32[]{:S(2)}) async-start(), calls=%async_computation.25 | async-start | bytes 1310720 | tf_op jit(solution)/shard_map/reduce_scatter | solution.py:304
  523.7 138.9 %reduce-scatter.29.cloned.1.call-start = ((), (), s32[]{:S(2)}) async-start(), calls=%async_computation.40 | async-start | bytes 1310720 | tf_op jit(solution)/shard_map/reduce_scatter | solution.py:341
  666.9 263.0 %all-gather.16.cloned.1.call-start = ((), (), s32[]{:S(2)}) async-start(), calls=%async_computation.26 | async-start | bytes 1310720 | tf_op jit(solution)/shard_map/all_gather | solution.py:313
  675.5 260.6 %all-gather.28.cloned.1.call-start = ((), (), s32[]{:S(2)}) async-start(), calls=%async_computation.35 | async-start | bytes 1310720 | tf_op jit(solution)/shard_map/all_gather | solution.py:332
  686.7 262.0 %reduce-scatter.31.cloned.1.call-start = ((), (), s32[]{:S(2)}) async-start(), calls=%async_computation.42 | async-start | bytes 1310720 | tf_op jit(solution)/shard_map/reduce_scatter | solution.py:372
  929.9 73.4 %reduce-scatter.25.cloned.1.call-start = ((), (), s32[]{:S(2)}) async-start(), calls=%async_computation.36 | async-start | bytes 1310720 | tf_op jit(solution)/shard_map/reduce_scatter | solution.py:341
  945.1 79.6 %all-gather.30.cloned.1.call-start = ((), (), s32[]{:S(2)}) async-start(), calls=%async_computation.37 | async-start | bytes 1310720 | tf_op jit(solution)/shard_map/all_gather | solution.py:353
  1007.8 296.0 %reduce-scatter.27.cloned.1.call-start = ((), (), s32[]{:S(2)}) async-start(), calls=%async_computation.38 | async-start | bytes 1310720 | tf_op jit(solution)/shard_map/reduce_scatter | solution.py:372
  1259.6 166.3 %reduce-scatter.39.cloned.1.call-start = ((), (), s32[]{:S(2)}) async-start(), calls=%async_computation.46 | async-start | bytes 36864 | tf_op jit(solution)/shard_map/reduce_scatter | solution.py:428
  1263.2 162.7 %all-reduce.17.cloned.1.call-start = ((), (), s32[]{:S(2)}) async-start(), calls=%async_computation.51 | async-start | bytes 524288 | tf_op jit(solution)/shard_map/psum | solution.py:434
  1270.6 171.9 %reduce-scatter.47.cloned.1.call-start = ((), (), s32[]{:S(2)}) async-start(), calls=%async_computation.50 | async-start | bytes 3244032 | tf_op jit(solution)/shard_map/reduce_scatter | solution.py:432
  1275.7 242.2 %reduce-scatter.45.cloned.1.call-start = ((), (), s32[]{:S(2)}) async-start(), calls=%async_computation.49 | async-start | bytes 3244032 | tf_op jit(solution)/shard_map/reduce_scatter | solution.py:431
  1280.8 312.6 %reduce-scatter.43.cloned.1.call-start = ((), (), s32[]{:S(2)}) async-start(), calls=%async_computation.48 | async-start | bytes 3244032 | tf_op jit(solution)/shard_map/reduce_scatter | solution.py:430
  1286.0 373.9 %reduce-scatter.41.cloned.1.call-start = ((), (), s32[]{:S(2)}) async-start(), calls=%async_computation.47 | async-start | bytes 1179648 | tf_op jit(solution)/shard_map/reduce_scatter | solution.py:429
  1291.5 435.0 %reduce-scatter.33.cloned.1.call-start = ((), (), s32[]{:S(2)}) async-start(), calls=%async_computation.43 | async-start | bytes 1179648 | tf_op jit(solution)/shard_map/reduce_scatter | solution.py:425
  1296.9 495.8 %reduce-scatter.35.cloned.1.call-start = ((), (), s32[]{:S(2)}) async-start(), calls=%async_computation.44 | async-start | bytes 1179648 | tf_op jit(solution)/shard_map/reduce_scatter | solution.py:426
  1297.4 562.1 %reduce-scatter.37.cloned.1.call-start = ((), (), s32[]{:S(2)}) async-start(), calls=%async_computation.45 | async-start | bytes 1179648 | tf_op jit(solution)/shard_map/reduce_scatter | solution.py:427
  1341.2 83.9 %all-to-all-start.3 = ((bf16[8,16,1024]{2,1,0:T(8,128)(2,1)}), bf16[8,16,1024]{2,1,0:T(8,128)(2,1)S(1)}, u32[]{:S(2)}, u32[]{:S(2)}) async-start(bf16[8,16,1024]{2,1,0:T(8,128)(2,1)} %bitcast.48), calls=%async_computation.7 | async-start | bytes 524288 | tf_op jit(solution)/shard_map/all_to_all | solution.py:386
  (246 other events, 5926.6 us)
Sparse Core Ops, SparseCore 0:
  54.9 14.0 all-gather.13
  128.2 14.0 all-gather.23
  458.1 22.1 reduce-scatter.20
  523.9 23.5 reduce-scatter.16
  639.5 23.0 reduce-scatter.28
  667.0 16.7 all-gather.33
  686.0 16.7 all-gather.15
  704.9 16.7 all-gather.27
  1007.9 16.7 all-gather.29
  1256.0 24.8 reduce-scatter.26
  1283.6 24.9 reduce-scatter.18
  1312.2 54.3 reduce-scatter.38
  1370.7 71.7 reduce-scatter.46
  1446.5 71.4 reduce-scatter.44
  1521.9 71.3 reduce-scatter.42
  1597.2 62.6 reduce-scatter.40
  1664.1 62.3 reduce-scatter.32
  1730.3 62.2 reduce-scatter.34
  1797.0 62.4 reduce-scatter.36
Sparse Core Ops, SparseCore 1:
  460.4 44.9 all-gather.17
  507.4 15.8 all-gather.25
  525.1 43.1 all-gather.19
  570.4 14.8 all-gather.31
  587.3 43.1 all-gather.21
  925.8 22.8 reduce-scatter.30
  951.1 24.8 reduce-scatter.22
  978.5 24.8 reduce-scatter.24
  1270.7 71.1 all-reduce.16
where the time goes:
time: 1890 us; the launch traced here: 1870 us
  waiting for transfers between devices  683 us (36%)
  matrix products  468 us (25%)
  blocking collectives  267 us (14%)
  local copies, waits for them, and re-layouts  223 us (12%)
  other arithmetic  161 us (9%)
  starting transfers between devices  39.8 us (2%)
  between operations  24.3 us (1%)
    dot_general x432, matrix products, highest(): jnp.dot(left, right, precision=lax.Precision.HIGHEST, preferred_element_t...  343 us
    squeeze x128, local copies, waits for them, and re-layouts, head_mix(): lax.scan(jax.checkpoint(memory_span), (first_layer, second_layer, blank_f...  115 us
    reduce_scatter x1, waiting for transfers between devices, per_device(): lax.psum_scatter(weight_totals[6], 'dp', scatter_dimension=0, tiled=True)  75.5 us
    reduce_scatter x1, waiting for transfers between devices, per_device(): lax.psum_scatter(weight_totals[5], 'dp', scatter_dimension=0, tiled=True)  75.4 us
    reduce_scatter x1, waiting for transfers between devices, per_device(): lax.psum_scatter(weight_totals[2], 'dp', scatter_dimension=0, tiled=True)  66.9 us
    reduce_scatter x1, waiting for transfers between devices, per_device(): lax.psum_scatter(weight_totals[0], 'dp', scatter_dimension=0, tiled=True)  66.6 us
    reduce_scatter x1, waiting for transfers between devices, per_device(): lax.psum_scatter(weight_totals[4], 'dp', scatter_dimension=0, tiled=True)  66.5 us
    reduce_scatter x1, waiting for transfers between devices, per_device(): lax.psum_scatter(weight_totals[1], 'dp', scatter_dimension=0, tiled=True)  66.2 us
  transfers between devices with their start and end apart: 36, of which 23 were waited for; matrix products, arithmetic and copies ran while one was open for 20% of the time, Pallas kernels for 0%

commit v1 on v0

v1 whole, which is shorter than its diff:
```python
from functools import partial

import jax
import jax.numpy as jnp
from jax import lax
from jax.experimental import pallas as pl
from jax.experimental.pallas import tpu as pltpu
from jax.sharding import Mesh
from jax.sharding import PartitionSpec as P

CH = 64
WINDOW = 256
EPS = 1e-06
NEG = -1e30
BF = jnp.bfloat16
F32 = jnp.float32


def _nn(a, b):
    return lax.dot_general(a, b, (((1,), (0,)), ((), ())), preferred_element_type=F32)


def _nt(a, b):
    return lax.dot_general(a, b, (((1,), (1,)), ((), ())), preferred_element_type=F32)


def _tn(a, b):
    return lax.dot_general(a, b, (((0,), (0,)), ((), ())), preferred_element_type=F32)


def _sig(v):
    return 1.0 / (1.0 + jnp.exp(-v))


def _scale_of(v):
    return lax.rsqrt(jnp.mean(v * v, axis=-1, keepdims=True) + EPS)


def _lane(shape, dim):
    return lax.broadcasted_iota(jnp.int32, shape, dim)


def _masks():
    rows = _lane((128, 128), 0)
    cols = _lane((128, 128), 1)
    return cols > rows, cols <= rows, (rows // CH) == (cols // CH)


def _scores(qs, near_keys, read_b, pkey, block, length, masks):
    older, newer, same_span = masks
    read_ok = same_span & (block * 128 + _lane((128, 128), 1) < length)
    parts = [_nt(qs, pkey), jnp.where(read_ok, _nt(qs, read_b), NEG)]
    for back, keys in near_keys:
        part = _nt(qs, keys)
        if back == 2:
            part = jnp.where(older, part, NEG)
        elif back == 0:
            part = jnp.where(newer, part, NEG)
        parts.append(part)
    return parts


def _spot(place, quarter):
    there = place ^ quarter
    return pl.multiple_of((((there & 1) << 1) | (there >> 1)) * 128, 128)


def _load_rows(place, length, qkv_ref, heads, qn_s, kn_s, qs_s, kb_s, v_s, vb_s, w_s, r_s):
    width = heads * 128
    for quarter in range(4):
        source = pl.ds(_spot(place, quarter), 128)
        here = pl.ds(quarter * 128, 128)
        live = (quarter * 128 + _lane((128, 1), 0) < length).astype(F32)
        rates = _sig(qkv_ref[source, 3 * width : 3 * width + 128])
        r_s[here, :] = rates
        for head in range(heads):
            at = slice(head * 128, (head + 1) * 128)
            q = qkv_ref[source, head * 128 : (head + 1) * 128]
            k = qkv_ref[source, width + head * 128 : width + (head + 1) * 128]
            v = qkv_ref[source, 2 * width + head * 128 : 2 * width + (head + 1) * 128]
            qn_s[here, at] = (q * _scale_of(q)).astype(BF)
            kn_s[here, at] = (k * _scale_of(k)).astype(BF)
            qs_s[here, at] = (q * (128 ** (-0.5))).astype(BF)
            kb_s[here, at] = k.astype(BF)
            v_s[here, at] = v
            vb_s[here, at] = v.astype(BF)
            weighting = rates[:, 3 * head : 3 * head + 1] * live * (2.0 / (CH * 128))
            w_s[here, at] = jnp.broadcast_to(weighting, (128, 128))


def _fwd_kernel(
    heads,
    where_ref,
    qkv_ref,
    pk_ref,
    pv_ref,
    m1_ref,
    m2_ref,
    mixed_ref,
    reads_ref,
    lse_ref,
    states_ref,
    qn_s,
    kn_s,
    qs_s,
    kb_s,
    v_s,
    vb_s,
    w_s,
    r_s,
):
    place = where_ref[0]
    length = where_ref[1]
    _load_rows(place, length, qkv_ref, heads, qn_s, kn_s, qs_s, kb_s, v_s, vb_s, w_s, r_s)
    carry = [
        [m1_ref[h], m2_ref[h], jnp.zeros((128, 128), F32), jnp.zeros((128, 128), F32)]
        for h in range(heads)
    ]
    for span in range(8):
        rows = slice(span * CH, (span + 1) * CH)
        means = jnp.mean(r_s[rows, :], axis=0, keepdims=True)
        for head in range(heads):
            at = slice(head * 128, (head + 1) * 128)
            first, second, s1, s2 = carry[head]
            first_b, second_b = first.astype(BF), second.astype(BF)
            states_ref[span, 0, head] = first_b
            states_ref[span, 1, head] = second_b
            states_ref[span, 2, head] = s1.astype(BF)
            states_ref[span, 3, head] = s2.astype(BF)
            kn = kn_s[rows, at]
            qn = qn_s[rows, at]
            both = _nn(jnp.concatenate([kn, qn], axis=0), first_b)
            both = both * _sig(both) if span == 7 else both
            if span < 7:
                pre = both[:CH]
                sig = _sig(both)
                act_both = both * sig
                sig_k = sig[:CH]
            else:
                act_both = both
            out_both = _nn(act_both.astype(BF), second_b)
            reads_ref[rows, at] = out_both[CH:].astype(BF)
            if span < 7:
                act = act_both[:CH]
                miss = (out_both[:CH] - v_s[rows, at]) * w_s[rows, at]
                miss_b = miss.astype(BF)
                grad_second = _tn(act.astype(BF), miss_b)
                grad_pre = _nt(miss_b, second_b) * sig_k * (1.0 + pre * (1.0 - sig_k))
                grad_first = _tn(kn, grad_pre.astype(BF))
                eta = means[:, 3 * head + 1 : 3 * head + 2]
                keep = 1.0 - 0.5 * means[:, 3 * head + 2 : 3 * head + 3]
                s1 = eta * s1 - grad_first
                s2 = eta * s2 - grad_second
                carry[head] = [keep * first + s1, keep * second + s2, s1, s2]
    masks = _masks()
    for block in range(4):
        rows = slice(block * 128, (block + 1) * 128)
        target = pl.ds(_spot(place, block), 128)
        lse_all = jnp.zeros((128, 128), F32)
        for head in range(heads):
            at = slice(head * 128, (head + 1) * 128)
            qs = qs_s[rows, at]
            near = [
                (back, slice((block - back) * 128, (block - back + 1) * 128))
                for back in (2, 1, 0)
                if block - back >= 0
            ]
            read_b = reads_ref[rows, at]
            parts = _scores(
                qs, [(b, kb_s[r, at]) for b, r in near], read_b, pk_ref[head], block, length, masks
            )
            top = jnp.max(parts[0], axis=1, keepdims=True)
            wide = parts[1]
            for part in parts[2:]:
                wide = jnp.maximum(wide, part)
            top = jnp.maximum(top, jnp.max(wide, axis=1, keepdims=True))
            exps = [jnp.exp(part - top) for part in parts]
            wide = exps[1]
            for part in exps[2:]:
                wide = wide + part
            total = jnp.sum(exps[0], axis=1, keepdims=True) + jnp.sum(wide, axis=1, keepdims=True)
            acc = _nn(exps[0].astype(BF), pv_ref[head]) + _nn(exps[1].astype(BF), read_b)
            for (_, r), part in zip(near, exps[2:]):
                acc = acc + _nn(part.astype(BF), vb_s[r, at])
            mixed_ref[target, at] = (acc / total).astype(BF)
            lse_all = jnp.where(
                _lane((128, 128), 1) == head, jnp.broadcast_to(top + jnp.log(total), (128, 128)), lse_all
            )
        lse_ref[rows, :] = lse_all


def _bwd_kernel(
    heads,
    where_ref,
    qkv_ref,
    pk_ref,
    pv_ref,
    mixed_ref,
    reads_ref,
    lse_ref,
    states_ref,
    dmix_ref,
    dqkv_ref,
    dz_ref,
    dpk_ref,
    dpv_ref,
    dm1_ref,
    dm2_ref,
    qn_s,
    kn_s,
    qs_s,
    kb_s,
    v_s,
    vb_s,
    w_s,
    r_s,
    dq_s,
    dk_s,
    dv_s,
    dr_s,
    dqn_s,
    dkn_s,
    dz_s,
):
    place = where_ref[0]
    length = where_ref[1]
    width = heads * 128
    _load_rows(place, length, qkv_ref, heads, qn_s, kn_s, qs_s, kb_s, v_s, vb_s, w_s, r_s)
    masks = _masks()
    scale = 128 ** (-0.5)
    for head in range(heads):
        at = slice(head * 128, (head + 1) * 128)
        dpk = jnp.zeros((16, 128), F32)
        dpv = jnp.zeros((16, 128), F32)
        dk = [jnp.zeros((128, 128), F32)] * 4
        dv = [jnp.zeros((128, 128), F32)] * 4
        for block in range(4):
            rows = slice(block * 128, (block + 1) * 128)
            source = pl.ds(_spot(place, block), 128)
            qs = qs_s[rows, at]
            near = [
                (back, slice((block - back) * 128, (block - back + 1) * 128))
                for back in (2, 1, 0)
                if block - back >= 0
            ]
            read_b = reads_ref[rows, at]
            parts = _scores(
                qs, [(b, kb_s[r, at]) for b, r in near], read_b, pk_ref[head], block, length, masks
            )
            lse = lse_ref[rows, head : head + 1]
            probs = [jnp.exp(part - lse) for part in parts]
            dout = dmix_ref[source, at]
            dout_b = dout.astype(BF)
            dot = jnp.sum(dout * mixed_ref[source, at].astype(F32), axis=1, keepdims=True)
            values = [pv_ref[head], read_b] + [vb_s[r, at] for _, r in near]
            keys = [pk_ref[head], read_b] + [kb_s[r, at] for _, r in near]
            ds_b = [
                (p * (_nt(dout_b, val) - dot)).astype(BF) for p, val in zip(probs, values)
            ]
            probs_b = [p.astype(BF) for p in probs]
            dq = _nn(ds_b[0], keys[0])
            for d, key in zip(ds_b[1:], keys[1:]):
                dq = dq + _nn(d, key)
            dq_s[rows, at] = dq * scale
            dpk = dpk + _tn(ds_b[0], qs)
            dpv = dpv + _tn(probs_b[0], dout_b)
            dr_s[rows, at] = _tn(ds_b[1], qs) + _tn(probs_b[1], dout_b)
            for (back, _), d, p in zip(near, ds_b[2:], probs_b[2:]):
                dk[block - back] = dk[block - back] + _tn(d, qs)
                dv[block - back] = dv[block - back] + _tn(p, dout_b)
            if block >= 2:
                dk_s[(block - 2) * 128 : (block - 1) * 128, at] = dk[block - 2]
                dv_s[(block - 2) * 128 : (block - 1) * 128, at] = dv[block - 2]
        for block in (2, 3):
            rows = slice(block * 128, (block + 1) * 128)
            dk_s[rows, at] = dk[block]
            dv_s[rows, at] = dv[block]
        dpk_ref[head] = dpk
        dpv_ref[head] = dpv
    zero = jnp.zeros((128, 128), F32)
    carry = [[zero, zero, zero, zero] for _ in range(heads)]
    lanes = _lane((CH, 128), 1)
    for span in range(7, -1, -1):
        rows = slice(span * CH, (span + 1) * CH)
        means = jnp.mean(r_s[rows, :], axis=0, keepdims=True)
        dr_row = jnp.zeros((CH, 128), F32)
        live = (span * CH + _lane((CH, 1), 0) < length).astype(F32)
        for head in range(heads):
            at = slice(head * 128, (head + 1) * 128)
            a1, a2, b1, b2 = carry[head]
            first_b = states_ref[span, 0, head]
            second_b = states_ref[span, 1, head]
            kn = kn_s[rows, at]
            qn = qn_s[rows, at]
            dread_b = dr_s[rows, at].astype(BF)
            both = _nn(jnp.concatenate([kn, qn], axis=0), first_b)
            sig_both = _sig(both)
            act_both = both * sig_both
            slope_both = sig_both * (1.0 + both * (1.0 - sig_both))
            act_b = act_both.astype(BF)
            db_b = (_nt(dread_b, second_b) * slope_both[CH:]).astype(BF)
            if span == 7:
                dqn_s[rows, at] = _nt(db_b, first_b)
                dkn_s[rows, at] = jnp.zeros((CH, 128), F32)
                carry[head] = [_tn(qn, db_b), _tn(act_b[CH:], dread_b), zero, zero]
                continue
            eta = means[:, 3 * head + 1 : 3 * head + 2]
            keep = 1.0 - 0.5 * means[:, 3 * head + 2 : 3 * head + 3]
            pre, sig, slope = both[:CH], sig_both[:CH], slope_both[:CH]
            bend = sig * (1.0 - sig) * (2.0 + pre * (1.0 - 2.0 * sig))
            u_b = act_b[:CH]
            w = w_s[rows, at]
            e = _nn(u_b, second_b) - v_s[rows, at]
            m_b = (e * w).astype(BF)
            p = _nt(m_b, second_b)
            g_b = (p * slope).astype(BF)
            ds1 = b1 + a1
            ds2 = b2 + a2
            dg1_b = (-ds1).astype(BF)
            dg2_b = (-ds2).astype(BF)
            x1 = _nn(kn, dg1_b)
            dp_b = (x1 * slope).astype(BF)
            dm = _nn(dp_b, second_b) + _nn(u_b, dg2_b)
            de = dm * w
            de_b = de.astype(BF)
            du = _nt(m_b, dg2_b) + _nt(de_b, second_b)
            da = x1 * p * bend + du * slope
            da_b = da.astype(BF)
            back = _nt(jnp.concatenate([da_b, db_b], axis=0), first_b)
            dkn_s[rows, at] = _nt(g_b, dg1_b) + back[:CH]
            dqn_s[rows, at] = back[CH:]
            dv_s[rows, at] = dv_s[rows, at] - de
            new1 = keep * a1 + _tn(
                jnp.concatenate([kn, qn], axis=0), jnp.concatenate([da_b, db_b], axis=0)
            )
            new2 = (
                keep * a2
                + _tn(act_b, jnp.concatenate([de_b, dread_b], axis=0))
                + _tn(dp_b, m_b)
            )
            prev1 = states_ref[span, 2, head].astype(F32)
            prev2 = states_ref[span, 3, head].astype(F32)
            deta = jnp.sum(
                jnp.sum(ds1 * prev1 + ds2 * prev2, axis=0, keepdims=True), axis=1, keepdims=True
            )
            dkeep = jnp.sum(
                jnp.sum(a1 * first_b.astype(F32) + a2 * second_b.astype(F32), axis=0, keepdims=True),
                axis=1,
                keepdims=True,
            )
            dw = jnp.sum(dm * e, axis=1, keepdims=True) * live * (2.0 / (CH * 128))
            dr_row = jnp.where(lanes == 3 * head, jnp.broadcast_to(dw, (CH, 128)), dr_row)
            dr_row = jnp.where(
                lanes == 3 * head + 1, jnp.broadcast_to(deta * (1.0 / CH), (CH, 128)), dr_row
            )
            dr_row = jnp.where(
                lanes == 3 * head + 2, jnp.broadcast_to(dkeep * (-0.5 / CH), (CH, 128)), dr_row
            )
            carry[head] = [new1, new2, eta * ds1, eta * ds2]
        rates = r_s[rows, :]
        dz_s[rows, :] = dr_row * rates * (1.0 - rates)
    for head in range(heads):
        dm1_ref[head] = carry[head][0]
        dm2_ref[head] = carry[head][1]
    for quarter in range(4):
        source = pl.ds(_spot(place, quarter), 128)
        here = slice(quarter * 128, (quarter + 1) * 128)
        dz_ref[source, :] = dz_s[here, :].astype(BF)
        for head in range(heads):
            at = slice(head * 128, (head + 1) * 128)
            for part, grad_s, norm_s in ((0, dq_s, dqn_s), (1, dk_s, dkn_s)):
                col = slice(part * width + head * 128, part * width + (head + 1) * 128)
                raw = qkv_ref[source, col]
                inverse = _scale_of(raw)
                normed = raw * inverse
                dn = norm_s[here, at]
                inner = jnp.mean(dn * normed, axis=-1, keepdims=True)
                dqkv_ref[source, col] = (
                    grad_s[here, at] + inverse * (dn - normed * inner)
                ).astype(BF)
            col = slice(2 * width + head * 128, 2 * width + (head + 1) * 128)
            dqkv_ref[source, col] = dv_s[here, at].astype(BF)


def _row_scratch(heads):
    wide = heads * 128
    return [
        pltpu.VMEM((512, wide), BF),
        pltpu.VMEM((512, wide), BF),
        pltpu.VMEM((512, wide), BF),
        pltpu.VMEM((512, wide), BF),
        pltpu.VMEM((512, wide), F32),
        pltpu.VMEM((512, wide), BF),
        pltpu.VMEM((512, wide), F32),
        pltpu.VMEM((512, 128), F32),
    ]


_VM = pl.BlockSpec(memory_space=pltpu.VMEM)
_SM = pl.BlockSpec(memory_space=pltpu.SMEM)


def mix_forward(where, qkv, pk, pv, m1, m2):
    heads = pk.shape[0]
    wide = heads * 128
    return pl.pallas_call(
        partial(_fwd_kernel, heads),
        out_shape=(
            jax.ShapeDtypeStruct((512, wide), BF),
            jax.ShapeDtypeStruct((512, wide), BF),
            jax.ShapeDtypeStruct((512, 128), F32),
            jax.ShapeDtypeStruct((8, 4, heads, 128, 128), BF),
        ),
        in_specs=[_SM] + [_VM] * 5,
        out_specs=(_VM,) * 4,
        scratch_shapes=_row_scratch(heads),
        compiler_params=pltpu.CompilerParams(vmem_limit_bytes=48 * 1024 * 1024),
    )(where, qkv, pk, pv, m1, m2)


def mix_backward(where, qkv, pk, pv, mixed, reads, lse, states, dmix):
    heads = pk.shape[0]
    wide = heads * 128
    return pl.pallas_call(
        partial(_bwd_kernel, heads),
        out_shape=(
            jax.ShapeDtypeStruct((512, 3 * wide), BF),
            jax.ShapeDtypeStruct((512, 128), BF),
            jax.ShapeDtypeStruct((heads, 16, 128), F32),
            jax.ShapeDtypeStruct((heads, 16, 128), F32),
            jax.ShapeDtypeStruct((heads, 128, 128), F32),
            jax.ShapeDtypeStruct((heads, 128, 128), F32),
        ),
        in_specs=[_SM] + [_VM] * 8,
        out_specs=(_VM,) * 6,
        scratch_shapes=_row_scratch(heads)
        + [pltpu.VMEM((512, wide), F32)] * 6
        + [pltpu.VMEM((512, 128), F32)],
        compiler_params=pltpu.CompilerParams(vmem_limit_bytes=48 * 1024 * 1024),
    )(where, qkv, pk, pv, mixed, reads, lse, states, dmix)


DP = ("z", "x")


def _swap(value, axis):
    return lax.ppermute(value, axis, [(0, 1), (1, 0)])


PAIR = [(0, 1), (1, 0), (2, 3), (3, 2)]
MIDDLE = [(1, 2), (2, 1)]
OUTWARD = [(1, 0), (2, 3)]
INWARD = [(0, 1), (3, 2)]


def _line():
    return lax.axis_size("z") == 4


def _block_ids():
    depth = lax.axis_size("z")
    z = lax.axis_index("z")
    x = lax.axis_index("x")
    if not _line():
        return jnp.arange(2 * depth, dtype=jnp.int32)
    low_half = z < 2
    zs = jnp.stack([z, z ^ 1, jnp.where(low_half, 2, 1), jnp.where(low_half, 3, 0)])
    return jnp.concatenate([2 * zs + x, 2 * zs + (x ^ 1)]).astype(jnp.int32)


def _gather_rows(own):
    if not _line():
        return lax.all_gather(own, DP, axis=0)
    middle = (lax.axis_index("z") + 1) // 2 == 1
    pair = lax.ppermute(own, "z", PAIR)
    near = jnp.stack([own, pair])
    crossed = lax.ppermute(near, "z", MIDDLE)
    passed = lax.ppermute(crossed, "z", OUTWARD)
    far = jnp.where(middle, crossed, passed)
    return jnp.concatenate([near, far, _swap(near, "x"), _swap(far, "x")])


def _scatter_rows(keep, send):
    if not _line():
        whole = jnp.concatenate([keep, send.astype(F32)])
        return lax.psum_scatter(whole.astype(BF), DP, scatter_dimension=0).astype(F32)
    total = keep + _swap(send, "x").astype(F32)
    far = total[2:] + lax.ppermute(total[2:].astype(BF), "z", INWARD).astype(F32)
    crossed = lax.ppermute(far.astype(BF), "z", MIDDLE).astype(F32)
    pair = lax.ppermute((total[1] + crossed[1]).astype(BF), "z", PAIR).astype(F32)
    return total[0] + crossed[0] + pair


def _sum_all(value, axes):
    for axis in axes:
        size = lax.axis_size(axis)
        step = 1
        while step < size:
            value = value + lax.ppermute(value, axis, [(i, i ^ step) for i in range(size)])
            step *= 2
    return value


def _gather_slots(own):
    column = jnp.concatenate([own, _swap(own, "y")])
    return jnp.concatenate([column, _swap(column, "c")])


def _scatter_slots(keep, send):
    half = keep.shape[0] // 2
    total = keep + _swap(send, "c").astype(F32)
    return total[:half] + _swap(total[half:].astype(BF), "y").astype(F32)


def _dot(a, b, out=F32):
    return lax.dot_general(a, b, (((1,), (0,)), ((), ())), preferred_element_type=out)


def _dot_t(a, b, out=F32):
    return lax.dot_general(a, b, (((1,), (1,)), ((), ())), preferred_element_type=out)


def _dot_r(a, b, out=F32):
    return lax.dot_general(a, b, (((0,), (0,)), ((), ())), preferred_element_type=out)


def per_device(
    tokens,
    grad_output,
    query_weight,
    key_weight,
    value_weight,
    rates_weight,
    out_weight,
    gate_weight,
    up_weight,
    down_weight,
    norm1_gain,
    norm2_gain,
    persist_key,
    persist_value,
    memory_first,
    memory_second,
    seq_lengths,
    deal,
):
    devices = lax.axis_size("z") * lax.axis_size("x")
    dp_index = lax.axis_index("z") * lax.axis_size("x") + lax.axis_index("x")
    place = lax.axis_index("y") * 2 + lax.axis_index("c")
    seq_count = seq_lengths.shape[0]
    batches = seq_count // devices
    local_rows = tokens.shape[2]
    width = tokens.shape[3]
    quarter = local_rows * devices
    rows_of = query_weight.shape[0]
    head_cols = query_weight.shape[1]
    heads = persist_key.shape[0]
    rate_cols = rates_weight.shape[1]
    hidden_cols = gate_weight.shape[1]
    half = width // 2

    batch_of = deal // devices
    batch_ids = jnp.arange(batches, dtype=jnp.int32)
    batch_tokens = jnp.sum(
        jnp.where(batch_of[None, :] == batch_ids[:, None], seq_lengths[None, :], 0), axis=1
    ).astype(F32)
    batch_scale = jnp.sum(seq_lengths).astype(F32) / (batches * batch_tokens)
    my_seqs = [b * devices + dp_index for b in range(batches)]
    lengths = [seq_lengths[s] for s in my_seqs]
    scales = [batch_scale[batch_of[s]] for s in my_seqs]
    positions = place * quarter + jnp.arange(quarter, dtype=jnp.int32)
    lives = [(positions < n).astype(F32)[:, None] for n in lengths]

    ids = _block_ids()
    order = (ids[:, None] * rows_of + jnp.arange(rows_of, dtype=jnp.int32)[None, :]).reshape(width)
    shuffle = (jnp.arange(width, dtype=jnp.int32)[:, None] == order[None, :]).astype(BF)

    def deal_in(array, b):
        part = array[b * devices : (b + 1) * devices, 0]
        return lax.all_to_all(part, DP, split_axis=0, concat_axis=0, tiled=True).reshape(
            quarter, width
        )

    def deal_out(rows):
        plain = _dot_t(rows.astype(BF), shuffle, BF)
        return lax.all_to_all(
            plain.reshape(devices, local_rows, width), DP, split_axis=0, concat_axis=0, tiled=True
        )

    got_tokens = [deal_in(tokens, b) for b in range(batches)]

    extra = jnp.zeros((16, 3 * head_cols), BF)
    extra = extra.at[0, : rate_cols * rows_of].set(rates_weight.T.reshape(rate_cols * rows_of))
    extra = extra.at[1, :rows_of].set(norm1_gain).at[1, rows_of : 2 * rows_of].set(norm2_gain)
    packed = _gather_rows(
        jnp.concatenate(
            [jnp.concatenate([query_weight, key_weight, value_weight], axis=1), extra], axis=0
        )
    )
    rates_full = (
        packed[:, rows_of, : rate_cols * rows_of]
        .reshape(devices, rate_cols, rows_of)
        .transpose(0, 2, 1)
        .reshape(width, rate_cols)
    )
    project = jnp.concatenate(
        [
            packed[:, :rows_of].reshape(width, 3 * head_cols),
            jnp.pad(rates_full, ((0, 0), (0, 128 - rate_cols))),
        ],
        axis=1,
    )
    gain_one = packed[:, rows_of + 1, :rows_of].reshape(width).astype(F32)
    gain_two = packed[:, rows_of + 1, rows_of : 2 * rows_of].reshape(width).astype(F32)
    out_full = _gather_rows(out_weight).reshape(width, head_cols)
    gate_full = _gather_rows(gate_weight).reshape(width, hidden_cols)
    up_full = _gather_rows(up_weight).reshape(width, hidden_cols)
    down_full = _gather_rows(down_weight).reshape(width, hidden_cols)

    got_cots = [deal_in(grad_output, b) for b in range(batches)]

    span = range(batches)
    token_rows = [_dot(got_tokens[b], shuffle) for b in span]
    inverse_one = [lax.rsqrt(jnp.mean(t * t, axis=-1, keepdims=True) + EPS) for t in token_rows]
    normed_one = [t * i for t, i in zip(token_rows, inverse_one)]
    first = [_gather_slots((n * gain_one).astype(BF)) for n in normed_one]
    where = [jnp.stack([place, lengths[b]]).astype(jnp.int32) for b in span]
    projected = [_dot(first[b], project) for b in span]
    mixes = [
        mix_forward(where[b], projected[b], persist_key, persist_value, memory_first, memory_second)
        for b in span
    ]
    mixed = [m[0] for m in mixes]
    attended = [
        _scatter_slots(
            _dot_t(mixed[b][: 2 * quarter], out_full), _dot_t(mixed[b][2 * quarter :], out_full, BF)
        )
        for b in span
    ]
    residual = [token_rows[b] + attended[b] for b in span]
    inverse_two = [lax.rsqrt(jnp.mean(r * r, axis=-1, keepdims=True) + EPS) for r in residual]
    normed_two = [r * i for r, i in zip(residual, inverse_two)]
    second = [_gather_slots((n * gain_two).astype(BF)) for n in normed_two]
    cot_rows = [
        _dot(got_cots[b], shuffle) * scales[b] * lives[b] for b in span
    ]
    cot_full = [_gather_slots(c.astype(BF)) for c in cot_rows]

    gate_grad, up_grad, hidden = [], [], []
    for b in span:
        gate_pre = _dot(second[b], gate_full)
        up_pre = _dot(second[b], up_full)
        hidden_grad = _dot(cot_full[b], down_full)
        gate_sig = jax.nn.sigmoid(gate_pre)
        hidden.append((gate_pre * gate_sig * up_pre).astype(BF))
        gate_grad.append(
            (hidden_grad * up_pre * gate_sig * (1.0 + gate_pre * (1.0 - gate_sig))).astype(BF)
        )
        up_grad.append((hidden_grad * gate_pre * gate_sig).astype(BF))
    two_grad = [
        _scatter_slots(
            _dot_t(gate_grad[b][: 2 * quarter], gate_full)
            + _dot_t(up_grad[b][: 2 * quarter], up_full),
            (
                _dot_t(gate_grad[b][2 * quarter :], gate_full)
                + _dot_t(up_grad[b][2 * quarter :], up_full)
            ).astype(BF),
        )
        for b in span
    ]
    scaled_two = [g * gain_two for g in two_grad]
    residual_grad = [
        cot_rows[b]
        + inverse_two[b]
        * (
            scaled_two[b]
            - normed_two[b] * jnp.mean(scaled_two[b] * normed_two[b], axis=-1, keepdims=True)
        )
        for b in span
    ]
    mixer_cot = [_gather_slots(r.astype(BF)) for r in residual_grad]
    mixed_grad = [_dot(mixer_cot[b], out_full) for b in span]
    backs = [
        mix_backward(
            where[b], projected[b], persist_key, persist_value, *mixes[b], mixed_grad[b]
        )
        for b in span
    ]
    feed = [
        _scatter_slots(
            _dot_t(hidden[b][: 2 * quarter], down_full),
            _dot_t(hidden[b][2 * quarter :], down_full, BF),
        )
        for b in span
    ]
    layer_out = [deal_out(lives[b] * (residual[b] + feed[b])) for b in span]

    def weight_grad(rows, grads):
        rows = jnp.concatenate(rows)
        grads = jnp.concatenate(grads)
        cols = grads.shape[1]
        keep = _dot_r(rows[:, :half], grads).reshape(devices // 2, rows_of, cols)
        send = _dot_r(rows[:, half:], grads, BF).reshape(devices // 2, rows_of, cols)
        return _scatter_rows(keep, send)

    down_total = weight_grad(cot_full, hidden)
    gate_total = weight_grad(second, gate_grad)
    up_total = weight_grad(second, up_grad)
    out_total = weight_grad(mixer_cot, mixed)

    one_grad = [
        _scatter_slots(
            _dot_t(backs[b][0][: 2 * quarter], project[:, : 3 * head_cols])
            + _dot_t(backs[b][1][: 2 * quarter], project[:, 3 * head_cols :]),
            (
                _dot_t(backs[b][0][2 * quarter :], project[:, : 3 * head_cols])
                + _dot_t(backs[b][1][2 * quarter :], project[:, 3 * head_cols :])
            ).astype(BF),
        )
        for b in span
    ]
    scaled_one = [g * gain_one for g in one_grad]
    token_grad = [
        residual_grad[b]
        + inverse_one[b]
        * (
            scaled_one[b]
            - normed_one[b] * jnp.mean(scaled_one[b] * normed_one[b], axis=-1, keepdims=True)
        )
        for b in span
    ]
    grad_tokens = [deal_out(t) for t in token_grad]

    rows = jnp.concatenate(first)
    project_grad = jnp.concatenate([backs[b][0] for b in span])
    rate_grad = jnp.concatenate([backs[b][1] for b in span])
    rate_total = (
        _dot_r(rate_grad, rows)[:rate_cols]
        .reshape(rate_cols, devices, rows_of)
        .transpose(1, 0, 2)
        .reshape(devices, 1, rate_cols * rows_of)
    )
    rate_total = jnp.pad(
        rate_total, ((0, 0), (0, 15), (0, 3 * head_cols - rate_cols * rows_of))
    )
    keep = _dot_r(rows[:, :half], project_grad).reshape(devices // 2, rows_of, 3 * head_cols)
    send = _dot_r(rows[:, half:], project_grad, BF).reshape(devices // 2, rows_of, 3 * head_cols)
    packed_total = _scatter_rows(
        jnp.concatenate([keep, rate_total[: devices // 2]], axis=1),
        jnp.concatenate([send, rate_total[devices // 2 :].astype(BF)], axis=1),
    )
    project_total = packed_total[:rows_of]
    rates_total = (
        packed_total[rows_of, : rate_cols * rows_of].reshape(rate_cols, rows_of).transpose(1, 0)
    )

    memory = [sum(backs[b][i] for b in span) for i in (2, 3, 4, 5)]
    flat = jnp.concatenate([m.reshape(-1, 128) for m in memory])
    flat = _sum_all(flat, ("x", "z"))
    memory_out = []
    start = 0
    for m in memory:
        size = m.size // 128
        memory_out.append(flat[start : start + size].reshape(m.shape))
        start += size

    gains = jnp.stack(
        [
            sum(jnp.sum(one_grad[b] * normed_one[b], axis=0) for b in span),
            sum(jnp.sum(two_grad[b] * normed_two[b], axis=0) for b in span),
        ]
    ).reshape(2, devices, rows_of)
    place_of = (ids[:, None] == jnp.arange(devices, dtype=jnp.int32)[None, :]).astype(F32)
    gains = jnp.sum(gains[:, :, None, :] * place_of[None, :, :, None], axis=1)
    gains = _sum_all(gains.reshape(2 * devices, rows_of), ("c", "y", "x", "z")).reshape(2, width)

    return (
        jnp.concatenate(layer_out)[:, None],
        jnp.concatenate(grad_tokens)[:, None],
        project_total[:, :head_cols],
        project_total[:, head_cols : 2 * head_cols],
        project_total[:, 2 * head_cols :],
        rates_total,
        out_total,
        gate_total,
        up_total,
        down_total,
        gains[0],
        gains[1],
        memory_out[0],
        memory_out[1],
        memory_out[2],
        memory_out[3],
    )


def solution(mesh):
    sizes = mesh.devices.shape
    fine = Mesh(mesh.devices.reshape(sizes[0] // 2, 2, 2, sizes[1] // 2), ("z", "x", "y", "c"))
    tensor = ("y", "c")
    return jax.shard_map(
        per_device,
        mesh=fine,
        in_specs=(
            P(None, tensor, DP, None),
            P(None, tensor, DP, None),
            P(DP, tensor),
            P(DP, tensor),
            P(DP, tensor),
            P(DP, tensor),
            P(DP, tensor),
            P(DP, tensor),
            P(DP, tensor),
            P(DP, tensor),
            P(DP),
            P(DP),
            P(tensor, None, None),
            P(tensor, None, None),
            P(tensor, None, None),
            P(tensor, None, None),
            P(),
            P(),
        ),
        out_specs=(
            P(None, tensor, DP, None),
            P(None, tensor, DP, None),
            P(DP, tensor),
            P(DP, tensor),
            P(DP, tensor),
            P(DP, tensor),
            P(DP, tensor),
            P(DP, tensor),
            P(DP, tensor),
            P(DP, tensor),
            P(),
            P(),
            P(tensor, None, None),
            P(tensor, None, None),
            P(tensor, None, None),
            P(tensor, None, None),
        ),
        check_vma=False,
    )
```

time: 1890 us -> 518 us (0.27)
  waiting for transfers between devices: 683 us -> 141 us
  matrix products: 468 us -> 60.6 us
  blocking collectives: 267 us -> 0 us
  local copies, waits for them, and re-layouts: 223 us -> 50.7 us
  starting transfers between devices: 39.8 us -> 155 us
  other arithmetic: 161 us -> 50.2 us
  Pallas kernels: 0 us -> 44.4 us
    reduce_scatter x16 -> x0, waiting for transfers between devices: 520 us -> none  [the longest x1 75.5 us: per_device(): lax.psum_scatter(weight_totals[6], 'dp', scatter_dimension=0, tiled=True)]
    dot_general x484 -> x53, matrix products: 468 us -> 60.6 us  [the longest x14 28.9 us: _dot(): lax.dot_general(a, b, (((1,), (0,)), ((), ())), preferred_element_type=out)]
    all_gather x7 -> x0, blocking collectives: 191 us -> none  [the longest x1 33.2 us: per_device(): lax.all_gather(out_weight, 'dp', axis=0, tiled=True)]
    ppermute x0 -> x85, waiting for transfers between devices: none -> 124 us  [the longest x47 95 us: _swap(): return lax.ppermute(value, axis, [(0, 1), (1, 0)])]
    all_gather x11 -> x0, waiting for transfers between devices: 112 us -> none  [the longest x1 45.2 us: per_device(): lax.all_gather(down_weight, 'dp', axis=0, tiled=True)]
    squeeze x128 -> x3, local copies, waits for them, and re-layouts: 115 us -> 4.33 us  [the longest x2 3.73 us: deal_in(): part = array[b * devices:(b + 1) * devices, 0]]
    ppermute x0 -> x85, starting transfers between devices: none -> 106 us  [the longest x47 37.9 us: _swap(): return lax.ppermute(value, axis, [(0, 1), (1, 0)])]
    psum x2 -> x0, blocking collectives: 75.9 us -> none  [the longest x1 38.1 us: per_device(): lax.psum((memory_totals[0], memory_totals[1], memory_totals[2], memory_to...]
  transfers between devices with their start and end apart: 36 -> 93, of which waited for: 23 -> 30; matrix products, arithmetic and copies ran while one was open for 20% -> 30% of each run, Pallas kernels for 0% -> 9%
where the time goes in v1:
time: 518 us; the launch traced here: 510 us
  starting transfers between devices  155 us (30%)
  waiting for transfers between devices  141 us (27%)
  matrix products  60.6 us (12%)
  local copies, waits for them, and re-layouts  50.7 us (10%)
  other arithmetic  50.2 us (10%)
  Pallas kernels  44.4 us (9%)
  between operations  7.83 us (2%)
    ppermute x47, waiting for transfers between devices, _swap(): return lax.ppermute(value, axis, [(0, 1), (1, 0)])  95 us
    ppermute x47, starting transfers between devices, _swap(): return lax.ppermute(value, axis, [(0, 1), (1, 0)])  37.9 us
    dot_general x14, matrix products, _dot(): lax.dot_general(a, b, (((1,), (0,)), ((), ())), preferred_element_type=out)  28.9 us
    all_to_all x4, starting transfers between devices, deal_out(): lax.all_to_all(plain.reshape(devices, local_rows, width), DP, split_axis=...  27.3 us
    pallas_call x2, Pallas kernels, mix_backward(): pl.pallas_call(partial(_bwd_kernel, heads), out_shape=(jax.ShapeDtypeStru...  25.4 us
    unnamed x226, local copies, waits for them, and re-layouts  25.3 us
    all_to_all x4, starting transfers between devices, deal_in(): lax.all_to_all(part, DP, split_axis=0, concat_axis=0, tiled=True)  21.5 us
    dot_general x28, matrix products, _dot_t(): lax.dot_general(a, b, (((1,), (1,)), ((), ())), preferred_element_type=out)  20.3 us
  transfers between devices with their start and end apart: 93, of which 30 were waited for; matrix products, arithmetic and copies ran while one was open for 30% of the time, Pallas kernels for 9%

profile of v1, /device:TPU:0, one launch (start us, length us, event | category | flops | bytes accessed | tf_op | source)
XLA Modules:
  0.0 510.3 jit_solution(8372025995780765303)
XLA Ops:
  13.7 4.8 all-to-all-start.2
  47.3 9.3 %all-to-all-start.4 = ((bf16[8,16,1024]{2,1,0:T(8,128)(2,1)}), bf16[8,16,1024]{2,1,0:T(8,128)(2,1)S(1)}, u32[]{:S(2)}, u32[]{:S(2)}) async-start(bf16[8,16,1024]{2,1,0:T(8,128)(2,1)} %get-tuple-element.145), calls=%async_computation.4 | async-start | bytes 524288 | tf_op jit(solution)/shard_map/all_to_all | solution.py:580
  60.6 6.0 %all-to-all-done.4 = bf16[8,16,1024]{2,1,0:T(8,128)(2,1)S(1)} async-done(((bf16[8,16,1024]{2,1,0:T(8,128)(2,1)}), bf16[8,16,1024]{2,1,0:T(8,128)(2,1)S(1)}, u32[]{:S(2)}, u32[]{:S(2)}) %all-to-all-start.4) | async-done | bytes 262176 | tf_op jit(solution)/shard_map/all_to_all | solution.py:580
  109.7 7.8 %collective-permute-done.28 = bf16[2,128,704]{1,2,0:T(8,128)(2,1)S(1)} collective-permute-done((bf16[2,128,704]{1,2,0:T(8,128)(2,1)S(1)}, bf16[2,128,704]{1,2,0:T(8,128)(2,1)S(1)}, u32[]{:S(2)}, u32[]{:S(2)}) %collective-permute-start.28) | collective-permute-done | bytes 360480 | tf_op jit(solution)/shard_map/ppermute | solution.py:478
  131.3 14.2 %collective-permute-done.30 = bf16[2,128,704]{1,2,0:T(8,128)(2,1)} collective-permute-done((bf16[2,128,704]{1,2,0:T(8,128)(2,1)}, bf16[2,128,704]{1,2,0:T(8,128)(2,1)}, u32[]{:S(2)}, u32[]{:S(2)}) %collective-permute-start.30) | collective-permute-done | bytes 360480 | tf_op jit(solution)/shard_map/ppermute | solution.py:447
  146.6 7.9 %collective-permute-done.4 = bf16[2,144,768]{2,1,0:T(8,128)(2,1)S(1)} collective-permute-done((bf16[2,144,768]{2,1,0:T(8,128)(2,1)}, bf16[2,144,768]{2,1,0:T(8,128)(2,1)S(1)}, u32[]{:S(2)}, u32[]{:S(2)}) %collective-permute-start.4) | collective-permute-done | bytes 442400 | tf_op jit(solution)/shard_map/ppermute | solution.py:447
  159.6 5.3 %collective-permute-done.5 = bf16[128,1024]{1,0:T(8,128)(2,1)S(1)} collective-permute-done((bf16[128,1024]{1,0:T(8,128)(2,1)S(1)}, bf16[128,1024]{1,0:T(8,128)(2,1)S(1)}, u32[]{:S(2)}, u32[]{:S(2)}) %collective-permute-start.5) | collective-permute-done | bytes 262176 | tf_op jit(solution)/shard_map/ppermute | solution.py:447
  177.2 9.4 %shard_map.297 = (bf16[512,256]{1,0:T(8,128)(2,1)S(1)}, bf16[512,256]{1,0:T(8,128)(2,1)S(1)}, f32[512,128]{1,0:T(8,128)S(1)}, bf16[8,4,2,128,128]{4,3,2,1,0:T(8,128)(2,1)S(1)}) custom-call(s32[2]{0:T(128)S(1)} %pad_add_fusion.1.where_ref, f32[512,896]{1,0:T(8,128)S(1)} %fusion.95.qkv_ref, bf16[2,16,128]{2,1,0:T(8,128)(2,1)S(1)} %copy-done.6, ...), custom_call_target="tpu_custom_call" | custom-call | tf_op jit(solution)/shard_map/pallas_call | solution.py:406
  196.3 4.7 collective-permute-done.33
  201.1 5.2 %collective-permute-done.13 = bf16[128,1024]{1,0:T(8,128)(2,1)S(1)} collective-permute-done((bf16[128,1024]{1,0:T(8,128)(2,1)S(1)}, bf16[128,1024]{1,0:T(8,128)(2,1)S(1)}, u32[]{:S(2)}, u32[]{:S(2)}) %collective-permute-start.13) | collective-permute-done | bytes 262176 | tf_op jit(solution)/shard_map/ppermute | solution.py:447
  208.5 9.6 %shard_map.298 = (bf16[512,256]{1,0:T(8,128)(2,1)S(1)}, bf16[512,256]{1,0:T(8,128)(2,1)S(1)}, f32[512,128]{1,0:T(8,128)S(1)}, bf16[8,4,2,128,128]{4,3,2,1,0:T(8,128)(2,1)S(1)}) custom-call(s32[2]{0:T(128)S(1)} %pad_add_fusion.2.where_ref, f32[512,896]{1,0:T(8,128)S(1)} %fusion.94.qkv_ref, bf16[2,16,128]{2,1,0:T(8,128)(2,1)S(1)} %copy-done.6, ...), custom_call_target="tpu_custom_call" | custom-call | tf_op jit(solution)/shard_map/pallas_call | solution.py:406
  232.4 5.6 %collective-permute-done.37 = bf16[128,1024]{1,0:T(8,128)(2,1)S(1)} collective-permute-done((bf16[128,1024]{1,0:T(8,128)(2,1)S(1)}, bf16[128,1024]{1,0:T(8,128)(2,1)S(1)}, u32[]{:S(2)}, u32[]{:S(2)}) %collective-permute-start.37) | collective-permute-done | bytes 262176 | tf_op jit(solution)/shard_map/ppermute | solution.py:447
  243.9 5.6 %collective-permute-done.32 = bf16[128,1024]{1,0:T(8,128)(2,1)S(1)} collective-permute-done((bf16[128,1024]{1,0:T(8,128)(2,1)S(1)}, bf16[128,1024]{1,0:T(8,128)(2,1)S(1)}, u32[]{:S(2)}, u32[]{:S(2)}) %collective-permute-start.32) | collective-permute-done | bytes 262176 | tf_op jit(solution)/shard_map/ppermute | solution.py:447
  251.3 5.1 all-to-all-start.1
  282.0 8.7 %collective-permute-done.69 = bf16[4,128,704]{1,2,0:T(8,128)(2,1)S(1)} collective-permute-done((bf16[4,128,704]{1,2,0:T(8,128)(2,1)S(1)}, bf16[4,128,704]{1,2,0:T(8,128)(2,1)S(1)}, u32[]{:S(2)}, u32[]{:S(2)}) %collective-permute-start.69) | collective-permute-done | bytes 720928 | tf_op jit(solution)/shard_map/ppermute | solution.py:447
  291.8 14.4 %collective-permute-done.73 = bf16[4,128,704]{1,2,0:T(8,128)(2,1)S(1)} collective-permute-done((bf16[4,128,704]{1,2,0:T(8,128)(2,1)S(1)}, bf16[4,128,704]{1,2,0:T(8,128)(2,1)S(1)}, u32[]{:S(2)}, u32[]{:S(2)}) %collective-permute-start.73) | collective-permute-done | bytes 720928 | tf_op jit(solution)/shard_map/ppermute | solution.py:447
  312.3 8.8 %collective-permute-done.65 = bf16[4,128,704]{1,2,0:T(8,128)(2,1)S(1)} collective-permute-done((bf16[4,128,704]{1,2,0:T(8,128)(2,1)S(1)}, bf16[4,128,704]{1,2,0:T(8,128)(2,1)S(1)}, u32[]{:S(2)}, u32[]{:S(2)}) %collective-permute-start.65) | collective-permute-done | bytes 720928 | tf_op jit(solution)/shard_map/ppermute | solution.py:447
  334.7 4.6 collective-permute-done.45
  370.3 5.5 %collective-permute-start.68 = (bf16[128,704]{0,1:T(8,128)(2,1)}, bf16[128,704]{0,1:T(8,128)(2,1)S(1)}, u32[]{:S(2)}, u32[]{:S(2)}) collective-permute-start(bf16[128,704]{0,1:T(8,128)(2,1)} %fusion.208), channel_id=1, source_target_pairs={{0,8},{8,0},{16,24},{24,16},{1,9},{9,1},{17,25},{25,17},{2,10},{10... | collective-permute-start | bytes 540680 | tf_op jit(solution)/shard_map/ppermute | solution.py:490
  377.3 12.6 %shard_map.299 = (bf16[512,768]{1,0:T(8,128)(2,1)S(1)}, bf16[512,128]{1,0:T(8,128)(2,1)S(1)}, f32[2,16,128]{2,1,0:T(8,128)S(1)}, f32[2,16,128]{2,1,0:T(8,128)S(1...) custom-call(s32[2]{0:T(128)S(1)} %pad_add_fusion.1.where_ref, f32[512,896]{1,0:T(8,128)S(1)} %copy-done.1, ...), custom_call_target="tpu_custom_call" | custom-call | tf_op jit(solution)/shard_map/pallas_call | solution.py:424
  405.8 12.8 %shard_map.300 = (bf16[512,768]{1,0:T(8,128)(2,1)S(1)}, bf16[512,128]{1,0:T(8,128)(2,1)S(1)}, f32[2,16,128]{2,1,0:T(8,128)S(1)}, f32[2,16,128]{2,1,0:T(8,128)S(1...) custom-call(s32[2]{0:T(128)S(1)} %pad_add_fusion.2.where_ref, f32[512,896]{1,0:T(8,128)S(1)} %fusion.94.qkv_ref, ...), custom_call_target="tpu_custom_call" | custom-call | tf_op jit(solution)/shard_map/pallas_call | solution.py:424
  425.6 5.8 %collective-permute-done.61 = bf16[4,128,256]{2,1,0:T(8,128)(2,1)S(1)} collective-permute-done((bf16[4,128,256]{2,1,0:T(8,128)(2,1)S(1)}, bf16[4,128,256]{2,1,0:T(8,128)(2,1)S(1)}, u32[]{:S(2)}, u32[]{:S(2)}) %collective-permute-start.61) | collective-permute-done | bytes 262176 | tf_op jit(solution)/shard_map/ppermute | solution.py:447
  484.8 13.6 %all-to-all-start.5 = ((bf16[8,16,1024]{2,1,0:T(8,128)(2,1)}), bf16[8,16,1024]{2,1,0:T(8,128)(2,1)S(1)}, u32[]{:S(2)}, u32[]{:S(2)}) async-start(bf16[8,16,1024]{2,1,0:T(8,128)(2,1)} %bitcast.350), calls=%async_computation.5 | async-start | bytes 524288 | tf_op jit(solution)/shard_map/all_to_all | solution.py:586
  501.7 4.9 all-to-all-done.5
  (590 shorter events, 310.0 us)
Async XLA Ops:
  0.7 32.3 %collective-permute-start.7 = (bf16[128,256]{1,0:T(8,128)(2,1)}, bf16[128,256]{1,0:T(8,128)(2,1)}, u32[]{:S(2)}, u32[]{:S(2)}) collective-permute-start(bf16[128,256]{1,0:T(8,128)(2,1)} %param.30), channel_id=1, source_target_pairs={{0,8},{8,0},{16,24},{24,16},{1,9},{9,1},{17,25},{25,17},{2,10},{10... | collective-permute-start | bytes 196616 | tf_op jit(solution)/shard_map/ppermute | solution.py:475
  3.8 33.6 %collective-permute-start.16 = (bf16[128,704]{0,1:T(8,128)(2,1)}, bf16[128,704]{0,1:T(8,128)(2,1)S(1)}, u32[]{:S(2)}, u32[]{:S(2)}) collective-permute-start(bf16[128,704]{0,1:T(8,128)(2,1)} %param.31), channel_id=1, source_target_pairs={{0,8},{8,0},{16,24},{24,16},{1,9},{9,1},{17,25},{25,17},{2,10},{10... | collective-permute-start | bytes 540680 | tf_op jit(solution)/shard_map/ppermute | solution.py:475
  3.9 35.6 %collective-permute-start.21 = (bf16[128,704]{0,1:T(8,128)(2,1)}, bf16[128,704]{0,1:T(8,128)(2,1)S(1)}, u32[]{:S(2)}, u32[]{:S(2)}) collective-permute-start(bf16[128,704]{0,1:T(8,128)(2,1)} %param.32), channel_id=1, source_target_pairs={{0,8},{8,0},{16,24},{24,16},{1,9},{9,1},{17,25},{25,17},{2,10},{10... | collective-permute-start | bytes 540680 | tf_op jit(solution)/shard_map/ppermute | solution.py:475
  5.8 34.5 %collective-permute-start.26 = (bf16[128,704]{0,1:T(8,128)(2,1)}, bf16[128,704]{0,1:T(8,128)(2,1)S(1)}, u32[]{:S(2)}, u32[]{:S(2)}) collective-permute-start(bf16[128,704]{0,1:T(8,128)(2,1)} %param.33), channel_id=1, source_target_pairs={{0,8},{8,0},{16,24},{24,16},{1,9},{9,1},{17,25},{25,17},{2,10},{10... | collective-permute-start | bytes 540680 | tf_op jit(solution)/shard_map/ppermute | solution.py:475
  9.9 35.5 %collective-permute-start = (bf16[144,768]{1,0:T(8,128)(2,1)}, bf16[144,768]{1,0:T(8,128)(2,1)S(1)}, u32[]{:S(2)}, u32[]{:S(2)}) collective-permute-start(bf16[144,768]{1,0:T(8,128)(2,1)} %get-tuple-element.156), channel_id=1, source_target_pairs={{0,8},{8,0},{16,24},{24,16},{1,9},{9,1},{17,25},{25,17},{2,10},{10... | collective-permute-start | bytes 663560 | tf_op jit(solution)/shard_map/ppermute | solution.py:475
  13.7 33.6 %all-to-all-start.2 = ((bf16[8,16,1024]{2,1,0:T(8,128)(2,1)}), bf16[8,16,1024]{2,1,0:T(8,128)(2,1)}, u32[]{:S(2)}, u32[]{:S(2)}) async-start(bf16[8,16,1024]{2,1,0:T(8,128)(2,1)} %get-tuple-element.147), calls=%async_computation.2 | async-start | bytes 524288 | tf_op jit(solution)/shard_map/all_to_all | solution.py:580
  39.5 66.9 %collective-permute-start.19 = (bf16[2,128,704]{1,2,0:T(8,128)(2,1)}, bf16[2,128,704]{1,2,0:T(8,128)(2,1)}, u32[]{:S(2)}, u32[]{:S(2)}) collective-permute-start(bf16[2,128,704]{1,2,0:T(8,128)(2,1)} %pad_maximum_fusion.28), channel_id=1, source_target_pairs={{0,4},{4,0},{1,5},{5,1},{2,6},{6,2},{3,7},{7,3},{8,12},{12,8},{9,1... | collective-permute-start | bytes 1081352 | tf_op jit(solution)/shard_map/ppermute | solution.py:447
  40.3 45.5 %collective-permute-start.17 = (bf16[2,128,704]{1,2,0:T(8,128)(2,1)}, bf16[2,128,704]{1,2,0:T(8,128)(2,1)}, u32[]{:S(2)}, u32[]{:S(2)}) collective-permute-start(bf16[2,128,704]{1,2,0:T(8,128)(2,1)} %pad_maximum_fusion.28), channel_id=1, source_target_pairs={{8,16},{16,8},{9,17},{17,9},{10,18},{18,10},{11,19},{19,11},{12,20... | collective-permute-start | bytes 1081352 | tf_op jit(solution)/shard_map/ppermute | solution.py:477
  43.9 46.1 %collective-permute-start.22 = (bf16[2,128,704]{1,2,0:T(8,128)(2,1)}, bf16[2,128,704]{1,2,0:T(8,128)(2,1)}, u32[]{:S(2)}, u32[]{:S(2)}) collective-permute-start(bf16[2,128,704]{1,2,0:T(8,128)(2,1)} %pad_maximum_fusion.29), channel_id=1, source_target_pairs={{8,16},{16,8},{9,17},{17,9},{10,18},{18,10},{11,19},{19,11},{12,20... | collective-permute-start | bytes 1081352 | tf_op jit(solution)/shard_map/ppermute | solution.py:477
  78.8 49.0 %all-to-all-start.6 = ((bf16[8,16,1024]{2,1,0:T(8,128)(2,1)}), bf16[8,16,1024]{2,1,0:T(8,128)(2,1)S(1)}, u32[]{:S(2)}, u32[]{:S(2)}) async-start(bf16[8,16,1024]{2,1,0:T(8,128)(2,1)} %get-tuple-element.144), calls=%async_computation.6 | async-start | bytes 524288 | tf_op jit(solution)/shard_map/all_to_all | solution.py:580
  118.5 47.2 %collective-permute-start.20 = (bf16[2,128,704]{1,2,0:T(8,128)(2,1)}, bf16[2,128,704]{1,2,0:T(8,128)(2,1)}, u32[]{:S(2)}, u32[]{:S(2)}) collective-permute-start(bf16[2,128,704]{1,2,0:T(8,128)(2,1)} %get-tuple-element.121), channel_id=1, source_target_pairs={{0,4},{4,0},{1,5},{5,1},{2,6},{6,2},{3,7},{7,3},{8,12},{12,8},{9,1... | collective-permute-start | bytes 1081352 | tf_op jit(solution)/shard_map/ppermute | solution.py:447
  120.2 46.6 %collective-permute-start.25 = (bf16[2,128,704]{1,2,0:T(8,128)(2,1)}, bf16[2,128,704]{1,2,0:T(8,128)(2,1)}, u32[]{:S(2)}, u32[]{:S(2)}) collective-permute-start(bf16[2,128,704]{1,2,0:T(8,128)(2,1)} %get-tuple-element.125), channel_id=1, source_target_pairs={{0,4},{4,0},{1,5},{5,1},{2,6},{6,2},{3,7},{7,3},{8,12},{12,8},{9,1... | collective-permute-start | bytes 1081352 | tf_op jit(solution)/shard_map/ppermute | solution.py:447
  130.4 38.4 %collective-permute-start.49 = (bf16[128,1024]{1,0:T(8,128)(2,1)S(1)}, bf16[128,1024]{1,0:T(8,128)(2,1)S(1)}, u32[]{:S(2)}, u32[]{:S(2)}) collective-permute-start(bf16[128,1024]{1,0:T(8,128)(2,1)S(1)} %get-tuple-element.101), channel_id=1, source_target_pairs={{0,2},{2,0},{1,3},{3,1},{4,6},{6,4},{5,7},{7,5},{8,10},{10,8},{9,1... | collective-permute-start | bytes 786440 | tf_op jit(solution)/shard_map/ppermute | solution.py:447
  243.3 83.2 %collective-permute-start.44 = (bf16[128,1024]{1,0:T(8,128)(2,1)}, bf16[128,1024]{1,0:T(8,128)(2,1)}, u32[]{:S(2)}, u32[]{:S(2)}) collective-permute-start(bf16[128,1024]{1,0:T(8,128)(2,1)} %slice.751), channel_id=1, source_target_pairs={{0,2},{2,0},{1,3},{3,1},{4,6},{6,4},{5,7},{7,5},{8,10},{10,8},{9,1... | collective-permute-start | bytes 786440 | tf_op jit(solution)/shard_map/ppermute | solution.py:447
  251.3 91.9 %all-to-all-start.1 = ((bf16[8,16,1024]{2,1,0:T(8,128)(2,1)}), bf16[8,16,1024]{2,1,0:T(8,128)(2,1)}, u32[]{:S(2)}, u32[]{:S(2)}) async-start(bf16[8,16,1024]{2,1,0:T(8,128)(2,1)} %bitcast.347), calls=%async_computation.1 | async-start | bytes 524288 | tf_op jit(solution)/shard_map/all_to_all | solution.py:586
  278.0 43.1 %collective-permute-start.65 = (bf16[4,128,704]{1,2,0:T(8,128)(2,1)S(1)}, bf16[4,128,704]{1,2,0:T(8,128)(2,1)S(1)}, u32[]{:S(2)}, u32[]{:S(2)}) collective-permute-start(bf16[4,128,704]{1,2,0:T(8,128)(2,1)S(1)} %bitcast.337), channel_id=1, source_target_pairs={{0,4},{4,0},{1,5},{5,1},{2,6},{6,2},{3,7},{7,3},{8,12},{12,8},{9,1... | collective-permute-start | bytes 2162696 | tf_op jit(solution)/shard_map/ppermute | solution.py:447
  280.6 52.3 %collective-permute-start.40 = (bf16[128,1024]{1,0:T(8,128)(2,1)S(1)}, bf16[128,1024]{1,0:T(8,128)(2,1)S(1)}, u32[]{:S(2)}, u32[]{:S(2)}) collective-permute-start(bf16[128,1024]{1,0:T(8,128)(2,1)S(1)} %slice.752), channel_id=1, source_target_pairs={{0,2},{2,0},{1,3},{3,1},{4,6},{6,4},{5,7},{7,5},{8,10},{10,8},{9,1... | collective-permute-start | bytes 786440 | tf_op jit(solution)/shard_map/ppermute | solution.py:447
  290.8 37.7 %collective-permute-start.52 = (bf16[128,1024]{1,0:T(8,128)(2,1)S(1)}, bf16[128,1024]{1,0:T(8,128)(2,1)S(1)}, u32[]{:S(2)}, u32[]{:S(2)}) collective-permute-start(bf16[128,1024]{1,0:T(8,128)(2,1)S(1)} %slice.749), channel_id=1, source_target_pairs={{0,2},{2,0},{1,3},{3,1},{4,6},{6,4},{5,7},{7,5},{8,10},{10,8},{9,1... | collective-permute-start | bytes 786440 | tf_op jit(solution)/shard_map/ppermute | solution.py:447
  306.2 34.7 %collective-permute-start.70 = (bf16[2,128,704]{1,2,0:T(8,128)(2,1)S(1)}, bf16[2,128,704]{1,2,0:T(8,128)(2,1)S(1)}, u32[]{:S(2)}, u32[]{:S(2)}) collective-permute-start(bf16[2,128,704]{1,2,0:T(8,128)(2,1)S(1)} %slice.746), channel_id=1, source_target_pairs={{0,8},{24,16},{1,9},{25,17},{2,10},{26,18},{3,11},{27,19},{4,12},{... | collective-permute-start | bytes 1081352 | tf_op jit(solution)/shard_map/ppermute | solution.py:488
  340.2 35.6 %collective-permute-start.46 = (bf16[256,1024]{1,0:T(8,128)(2,1)}, bf16[256,1024]{1,0:T(8,128)(2,1)}, u32[]{:S(2)}, u32[]{:S(2)}) collective-permute-start(bf16[256,1024]{1,0:T(8,128)(2,1)} %pad_maximum_fusion.20), channel_id=1, source_target_pairs={{0,1},{1,0},{2,3},{3,2},{4,5},{5,4},{6,7},{7,6},{8,9},{9,8},{10,11... | collective-permute-start | bytes 1572872 | tf_op jit(solution)/shard_map/ppermute | solution.py:447
  362.3 33.6 %collective-permute-start.72 = (bf16[128,704]{0,1:T(8,128)(2,1)}, bf16[128,704]{0,1:T(8,128)(2,1)}, u32[]{:S(2)}, u32[]{:S(2)}) collective-permute-start(bf16[128,704]{0,1:T(8,128)(2,1)} %fusion.209), channel_id=1, source_target_pairs={{0,8},{8,0},{16,24},{24,16},{1,9},{9,1},{17,25},{25,17},{2,10},{10... | collective-permute-start | bytes 540680 | tf_op jit(solution)/shard_map/ppermute | solution.py:490
  365.4 32.4 %collective-permute-start.76 = (bf16[128,704]{0,1:T(8,128)(2,1)}, bf16[128,704]{0,1:T(8,128)(2,1)}, u32[]{:S(2)}, u32[]{:S(2)}) collective-permute-start(bf16[128,704]{0,1:T(8,128)(2,1)} %fusion.210), channel_id=1, source_target_pairs={{0,8},{8,0},{16,24},{24,16},{1,9},{9,1},{17,25},{25,17},{2,10},{10... | collective-permute-start | bytes 540680 | tf_op jit(solution)/shard_map/ppermute | solution.py:490
  402.8 45.4 %collective-permute-start.48 = (bf16[128,1024]{1,0:T(8,128)(2,1)S(1)}, bf16[128,1024]{1,0:T(8,128)(2,1)S(1)}, u32[]{:S(2)}, u32[]{:S(2)}) collective-permute-start(bf16[128,1024]{1,0:T(8,128)(2,1)S(1)} %slice.750), channel_id=1, source_target_pairs={{0,2},{2,0},{1,3},{3,1},{4,6},{6,4},{5,7},{7,5},{8,10},{10,8},{9,1... | collective-permute-start | bytes 786440 | tf_op jit(solution)/shard_map/ppermute | solution.py:447
  447.3 35.6 %collective-permute-start.84 = (f32[576,128]{1,0:T(8,128)}, f32[576,128]{1,0:T(8,128)}, u32[]{:S(2)}, u32[]{:S(2)}) collective-permute-start(f32[576,128]{1,0:T(8,128)} %add.496), channel_id=1, source_target_pairs={{0,16},{8,24},{16,0},{24,8},{1,17},{9,25},{17,1},{25,9},{2,18},{10... | collective-permute-start | bytes 884744 | tf_op jit(solution)/shard_map/ppermute | solution.py:499
  (167 other events, 1940.4 us)
